TPU v7x, 32 devices: a whole 2x2x4 slice. The times are simulated.
32 devices in a mesh: expert: 8 (over z, x), hidden: 4 (over y, core).
Axes of the slice: x: 2, y: 2, z: 4, core: 2. Of those that a mesh axis runs over, the one named last changes fastest.
Arguments:
- tokens: bfloat16 [16384, 512], P(('expert', 'hidden')), may hold values from -6 to 6
- lengths: int32 [32, 16], P(('expert', 'hidden')), may hold values from 1 to 256, 512 in all within a row
- task_ids: int32 [32, 16], P(('expert', 'hidden')), may hold values from 0 to 29
- routes: int32 [16384, 2], P(('expert', 'hidden')), may hold values from 0 to 7, all different within a row; in each aligned block of 512 rows (0 to 511, 512 to 1023, ...) at most 192 rows name the same one
- w_qkv: bfloat16 [512, 1536], P(('expert', 'hidden')), may hold values from -0.25 to 0.25
- w_attn_out: bfloat16 [512, 512], P(('expert', 'hidden')), may hold values from -1 to 1
- w_gate: bfloat16 [512, 240], P(('expert', 'hidden')), may hold values from -0.1875 to 0.1875
- ln1_gain: bfloat16 [512], P(('expert', 'hidden')), may hold values from 0.5 to 1.5
- ln1_bias: bfloat16 [512], P(('expert', 'hidden')), may hold values from -1 to 1
- ln2_gain: bfloat16 [512], P(('expert', 'hidden')), may hold values from 0.5 to 1.5
- ln2_bias: bfloat16 [512], P(('expert', 'hidden')), may hold values from -1 to 1
- w_in: bfloat16 [8, 512, 2048], P('expert', None, 'hidden'), may hold values from -0.25 to 0.25
- w_out: bfloat16 [8, 2048, 512], P('expert', 'hidden'), may hold values from -0.25 to 0.25
- cotangent: bfloat16 [16384, 512], P(('expert', 'hidden')), may hold values from -6 to 6
Outputs:
- layer_out: bfloat16 [16384, 512], P(('expert', 'hidden'))
- grad_tokens: float32 [16384, 512], P(('expert', 'hidden'))
- grad_w_qkv: float32 [512, 1536], P(('expert', 'hidden'))
- grad_w_attn_out: float32 [512, 512], P(('expert', 'hidden'))
- grad_w_gate: float32 [512, 240], P(('expert', 'hidden'))
- grad_ln1_gain: float32 [512], P(('expert', 'hidden'))
- grad_ln1_bias: float32 [512], P(('expert', 'hidden'))
- grad_ln2_gain: float32 [512], P(('expert', 'hidden'))
- grad_ln2_bias: float32 [512], P(('expert', 'hidden'))
- grad_w_in: float32 [8, 512, 2048], P('expert', None, 'hidden')
- grad_w_out: float32 [8, 2048, 512], P('expert', 'hidden')
Inputs may be any that keep to these rules, and one draw needn't show every extreme that they name: `lengths`: 16 sentences a pack, of 1 to 256 tokens, that fill its 512 tokens; the longest of each pack has exactly 256. `routes`: each token names 2 different experts; among the 512 tokens of one device no expert is named more than 192 times, and on some device some expert exactly 192 times.
All inputs are finite; a program needn't handle non-finite values.
Results may differ from a plain program's by a relative error of at most 0.015.
Values may be sent and summed in bfloat16 or wider, within the bound.
No kernel may reach another device: no remote copies, remote signals or barrier semaphores. Data moves between devices by JAX's collectives and lax.ppermute only.
A program may use at most 256 MiB of HBM per device.

v0:
```python
import functools

import jax
import jax.numpy as jnp
from jax import lax
from jax.experimental import pallas as pl
from jax.experimental.pallas import tpu as pltpu
from jax.sharding import PartitionSpec as P

HEADS = 8
HEAD_DIM = 64
EPS = 1e-05
NEG_FILL = -1e30
LANES = 128
BOTH = ("expert", "hidden")
F32 = jnp.float32
BF16 = jnp.bfloat16
VMEM_LIMIT = 56 * 1024 * 1024
SMALL_LIMIT = 8 * 1024 * 1024


def mm(left, right):
    return jnp.dot(left, right, preferred_element_type=F32)


def contract_last(left, right):
    return lax.dot_general(left, right, (((1,), (1,)), ((), ())), preferred_element_type=F32)


def contract_first(left, right):
    return lax.dot_general(left, right, (((0,), (0,)), ((), ())), preferred_element_type=F32)


def iota(shape, axis):
    return lax.broadcasted_iota(jnp.int32, shape, axis)


def iota_f(shape, axis):
    return iota(shape, axis).astype(F32)


def lane_sum(values):
    return jnp.sum(values, axis=1, keepdims=True)


def row_sum(values):
    return jnp.sum(values, axis=0, keepdims=True)


def norm_parts(values):
    middle = jnp.mean(values, axis=-1, keepdims=True)
    centred = values - middle
    spread = jnp.mean(centred * centred, axis=-1, keepdims=True)
    inverse = lax.rsqrt(spread + EPS)
    return centred * inverse, inverse


def norm_back(unit, inverse, gain, grad):
    scaled = grad * gain
    mean_one = jnp.mean(scaled, axis=-1, keepdims=True)
    mean_two = jnp.mean(scaled * unit, axis=-1, keepdims=True)
    return inverse * (scaled - mean_one - unit * mean_two)


def round_up(value, step):
    return (value + step - 1) // step * step


def call(kernel, outs, scratch, args, flops, smem=(), far_in=(), far_out=(), limit=VMEM_LIMIT):
    def spec(at):
        space = pltpu.SMEM if at in smem else pl.ANY if at in far_in else pltpu.VMEM
        return pl.BlockSpec(memory_space=space)

    def out_spec(at):
        return pl.BlockSpec(memory_space=pl.ANY if at in far_out else pltpu.VMEM)

    touched = sum(a.size * a.dtype.itemsize for a in args) + sum(
        o.size * o.dtype.itemsize for o in jax.tree.leaves(outs)
    )
    got = pl.pallas_call(
        kernel,
        out_shape=outs,
        in_specs=[spec(at) for at in range(len(args))],
        out_specs=[out_spec(at) for at in range(len(outs))] if isinstance(outs, list) else out_spec(0),
        scratch_shapes=scratch,
        compiler_params=pltpu.CompilerParams(vmem_limit_bytes=limit),
        cost_estimate=pl.CostEstimate(flops=1, bytes_accessed=1, transcendentals=0),
    )(*args)
    return list(got) if isinstance(outs, list) else got


def shape(dims, dtype):
    return jax.ShapeDtypeStruct(dims, dtype)


def slot_targets(cfg, routes_ref):
    count, experts = routes_ref.shape[1], cfg.experts
    both = jnp.zeros((8, count), F32)
    for at in (0, 1):
        both = jnp.where(iota((8, count), 0) == at, routes_ref[at : at + 1, :].astype(F32), both)
    routes = jnp.transpose(both)
    first, second = routes[:, 0:1], routes[:, 1:2]
    lane_e = iota_f((count, experts), 1)
    hot_one = jnp.where(lane_e == first, 1.0, 0.0)
    hot_two = jnp.where(lane_e == second, 1.0, 0.0)
    before = jnp.where(iota((count, count), 1) < iota((count, count), 0), 1.0, 0.0).astype(BF16)
    earlier = mm(before, (hot_one + hot_two).astype(BF16))
    target_one = first * cfg.cap + lane_sum(earlier * hot_one)
    target_two = second * cfg.cap + lane_sum(earlier * hot_two)
    return first, second, target_one, target_two


def prep_kernel(cfg, lens_ref, tasks_ref, routes_ref, cot_in, side_out, rows_out, sent_out, *scratch):
    experts, cap = cfg.experts, cfg.cap
    cot_ref, side_ref, rows_ref, sent_ref, in_sems, out_sems = scratch
    loads, stores = Copies(in_sems), Copies(out_sems)
    loads.start(cot_in, cot_ref)
    count = routes_ref.shape[1]
    sents = lens_ref.shape[1]
    lens = lens_ref[...].astype(F32)
    tasks = tasks_ref[...].astype(F32)
    down, across = iota((sents, sents), 0), iota((sents, sents), 1)
    ends_col = lane_sum(jnp.where(across <= down, lens, 0.0))
    ends_row = row_sum(jnp.where(across == down, ends_col, 0.0))
    passed = jnp.where(iota_f((count, sents), 0) >= ends_row, 1.0, 0.0)
    sentence = lane_sum(passed)
    task = lane_sum(jnp.where(iota_f((count, sents), 1) == sentence, tasks, 0.0))
    lane = iota((count, LANES), 1)
    first, second, target_one, target_two = slot_targets(cfg, routes_ref)
    side = jnp.where(lane == 0, target_one, 0.0)
    side = jnp.where(lane == 1, target_two, side)
    side = jnp.where(lane == 2, task * experts + first, side)
    side = jnp.where(lane == 3, task * experts + second, side)
    side = jnp.where(lane == 4, sentence, side)
    side = jnp.where(lane == 5, first, side)
    side = jnp.where(lane == 6, second, side)
    side_ref[...] = side
    stores.start(side_ref, side_out)
    turned = jnp.transpose(side)
    rows_ref[...] = turned[0:8, :]
    stores.start(rows_ref, rows_out)
    one_row, two_row = turned[0:1, :], turned[1:2, :]
    loads.finish()
    cot = cot_ref[...]
    for e in range(experts):
        at = iota_f((cap, count), 0) + float(e * cap)
        pick = jnp.where((at == one_row) | (at == two_row), 1.0, 0.0).astype(BF16)
        sent_ref[e // 2, e % 2] = mm(pick, cot).astype(BF16)
        stores.start(sent_ref.at[e // 2, e % 2], sent_out.at[e // 2, e % 2])
    stores.finish()


def pack_kernel(qkv_ref, attn_ref, gate_ref, *refs):
    vector_refs, out_ref = refs[:4], refs[4]
    rows = out_ref.shape[0]
    at = 0
    for ref in (qkv_ref, attn_ref):
        out_ref[:, at : at + ref.shape[1]] = ref[...]
        at += ref.shape[1]
    columns = gate_ref.shape[1]
    lanes = out_ref.shape[1] - at
    tile = columns // LANES * LANES
    out_ref[:, at : at + columns] = gate_ref[...]
    eye = iota((rows, rows), 0) == iota((rows, rows), 1)
    lane = iota((rows, lanes - tile), 1)
    last = out_ref[:, at + tile :].astype(F32)
    last = jnp.where(lane < columns - tile, last, 0.0)
    for i in range(4):
        column = lane_sum(jnp.where(eye, vector_refs[i][...].astype(F32), 0.0))
        last = jnp.where(lane == columns - tile + i, column, last)
    out_ref[:, at + tile :] = last.astype(BF16)


class Groups:
    def __init__(self, devices):
        bits = devices.bit_length() - 1
        mid = (bits - 1) // 2
        self.near = [1]
        self.mid = self.masks(1, mid)
        self.far = self.masks(1 + mid, bits - 1 - mid)
        self.devices = devices

    @staticmethod
    def masks(low, width):
        return [m << low for m in range(1 << width)]

    def owners(self):
        return [[n | b | c for c in self.far] for n in (0, 1) for b in self.mid]

    def swap(self, value, mask):
        return lax.ppermute(value, BOTH, [(i, i ^ mask) for i in range(self.devices)])

    def gather_far(self, shard):
        return jnp.concatenate([shard] + [self.swap(shard, m) for m in self.far[1:]], axis=0)

    def gather_near(self, far):
        mid = [far] + [self.swap(far, m) for m in self.mid[1:]]
        return mid + [self.swap(block, 1) for block in mid]


def add_kernel(parts, keep_ref, *refs):
    got, outs = refs[: len(refs) - parts], refs[len(refs) - parts :]
    rows = outs[0].shape[0]
    for i, out_ref in enumerate(outs):
        span = slice(i * rows, (i + 1) * rows)
        total = keep_ref[span, :].astype(F32)
        for ref in got:
            total = total + ref[span, :].astype(F32)
        out_ref[...] = total.astype(out_ref.dtype)


def add_parts(keep, got, parts):
    rows, columns = keep.shape
    outs = [shape((rows // parts, columns), F32 if i == 0 else BF16) for i in range(parts)]
    return call(
        functools.partial(add_kernel, parts), outs, [], [keep] + got, rows * columns * len(got), limit=SMALL_LIMIT
    )


def split_kernel(cfg, *refs):
    terms, outs = refs[:-7], refs[-7:]
    rows, width = outs[0].shape[0], outs[1].shape[1]

    def total(start, stop):
        value = terms[0][:, start:stop]
        for ref in terms[1:]:
            value = value + ref[:, start:stop].astype(F32)
        return value

    outs[0][...] = total(0, 3 * width)
    outs[1][...] = total(3 * width, 4 * width)
    outs[2][...] = total(4 * width, 4 * width + cfg.gate_columns)
    tile = 4 * width + cfg.gate_columns // LANES * LANES
    lane = cfg.gate_columns % LANES
    turned = jnp.transpose(total(tile, tile + LANES))
    for i in range(4):
        outs[3 + i][...] = turned[lane + i : lane + i + 1, :]


def gain_rows(full_ref, start, gate_columns):
    tile = start + gate_columns // LANES * LANES
    lane = gate_columns % LANES
    turned = jnp.transpose(full_ref[:, tile : tile + LANES].astype(F32))
    return [turned[lane + i : lane + i + 1, :] for i in range(4)]


def forward_kernel(cfg, me_ref, side_ref, rows_ref, tokens_ref, *refs):
    n, cap = cfg.experts, cfg.cap
    blocks, refs = refs[: cfg.blocks], refs[cfg.blocks :]
    outs, refs = refs[:6], refs[6:]
    even_out, odd_outs, refs = refs[0], refs[1 : 1 + n // 2], refs[1 + n // 2 :]
    full_ref, proj_ref, heads_ref, turned_ref, hidden_ref, gates_ref, send_all = refs[:7]
    rows_all, pick_ref_all, bias_ref, routed_ref, lse_ref, in_sems, out_sems = refs[7:]
    count, width = tokens_ref.shape
    me = me_ref[0]
    mine = me // cfg.hidden
    loads, stores = Copies(in_sems), Copies(out_sems)
    if len(blocks) == 1:
        loads.start(blocks[0], full_ref)
    else:
        for block_ref, masks in zip(blocks, cfg.owners):
            rows = block_ref.shape[0] // len(masks)
            for i, mask in enumerate(masks):
                at = pl.multiple_of((me ^ mask) * rows, rows)
                loads.start(block_ref.at[i * rows : (i + 1) * rows], full_ref.at[pl.ds(at, rows)])
    chunk = 512
    for c in range(count // chunk):
        span = slice(c * chunk, (c + 1) * chunk)
        bias_ref[span, :] = jnp.where(side_ref[span, 4:5] == rows_ref[4:5, :], 0.0, NEG_FILL)
        hidden_ref[span, :], _ = norm_parts(tokens_ref[span, :].astype(F32))
    for k in range(n):
        at = iota_f((cap, count), 0) + ((mine ^ k) * cap).astype(F32)
        pick = (at == rows_ref[0:1, :]) | (at == rows_ref[1:2, :])
        pick_ref_all[k * cap : (k + 1) * cap, :] = jnp.where(pick, 1.0, 0.0).astype(BF16)
    loads.finish()
    stores.start(full_ref, outs[0])
    gain_one, bias_one, gain_two, bias_two = gain_rows(full_ref, 4 * width, cfg.gate_columns)
    for c in range(count // chunk):
        span = slice(c * chunk, (c + 1) * chunk)
        routed_ref[span, :] = (hidden_ref[span, :] * gain_one + bias_one).astype(BF16)
    proj_ref[...] = mm(routed_ref[...], full_ref[:, : 3 * width]).astype(BF16)
    stores.start(proj_ref, outs[1])
    lse_ref[...] = jnp.zeros_like(lse_ref)
    lane = iota((1, LANES), 1)
    scale = HEAD_DIM ** (-0.5)
    block = 256

    def slab(i, carry):
        off = i * LANES
        keys = proj_ref[:, pl.ds(width + off, LANES)]
        values = proj_ref[:, pl.ds(2 * width + off, LANES)]
        halves = []
        for half in (0, 1):
            mine = jnp.where(lane // HEAD_DIM == half, 1.0, 0.0).astype(BF16)
            halves.append((keys * mine, values * mine))
        for r in range(count // block):
            span = slice(r * block, (r + 1) * block)
            queries = proj_ref[span, pl.ds(off, LANES)]
            total = jnp.zeros((block, LANES), F32)
            logs = lse_ref[span, :]
            for half, (key_half, value_half) in enumerate(halves):
                scores = contract_last(queries, key_half) * scale + bias_ref[span, :]
                highest = jnp.max(scores, axis=1, keepdims=True)
                expo = jnp.exp(scores - highest)
                sums = lane_sum(expo)
                probs = (expo * (1.0 / sums)).astype(BF16)
                total = total + mm(probs, value_half)
                logs = jnp.where(lane == 2 * i + half, highest + jnp.log(sums), logs)
            heads_ref[span, pl.ds(off, LANES)] = total.astype(BF16)
            lse_ref[span, :] = logs
        return carry

    for i in range(width // LANES):
        slab(i, 0)
    stores.start(heads_ref, outs[2])
    turned_ref[...] = jnp.transpose(lse_ref[...])[:HEADS, :]
    stores.start(turned_ref, outs[3])
    for c in range(count // chunk):
        span = slice(c * chunk, (c + 1) * chunk)
        attended = mm(heads_ref[span, :], full_ref[:, 3 * width : 4 * width])
        hidden = tokens_ref[span, :].astype(F32) + attended
        hidden_ref[span, :] = hidden
        unit, _ = norm_parts(hidden)
        routed = (unit * gain_two + bias_two).astype(BF16)
        routed_ref[span, :] = routed
        logits = mm(routed, full_ref[:, 4 * width :])
        column = iota_f(logits.shape, 1)
        one = lane_sum(jnp.where(column == side_ref[span, 2:3], logits, 0.0))
        two = lane_sum(jnp.where(column == side_ref[span, 3:4], logits, 0.0))
        top = jnp.maximum(one, two)
        expo_one, expo_two = jnp.exp(one - top), jnp.exp(two - top)
        both = expo_one + expo_two
        gates_ref[span, :] = jnp.where(
            lane == 0, expo_one / both, jnp.where(lane == 1, expo_two / both, 0.0)
        )
    stores.start(hidden_ref, outs[4])
    stores.start(gates_ref, outs[5])
    gate_lanes = round_up(cap, LANES)
    rows_all[...] = mm(pick_ref_all[...], routed_ref[...]).astype(BF16)
    for k in range(n):
        base = ((mine ^ k) * cap).astype(F32)
        out_ref = pick_ref(mine, k, even_out, odd_outs)
        stores.start(rows_all.at[k * cap : (k + 1) * cap], out_ref.at[0:cap])
        slot = iota_f((count, gate_lanes), 1) + base
        row = row_sum(
            jnp.where(slot == side_ref[:, 0:1], gates_ref[:, 0:1], 0.0)
            + jnp.where(slot == side_ref[:, 1:2], gates_ref[:, 1:2], 0.0)
        )
        put_split(send_all.at[k], 0, row)
        stores.start(send_all.at[k], out_ref.at[cap : cap + send_all.shape[1]])
    stores.finish()


def pick_ref(mine, k, even_ref, odd_refs):
    return odd_refs[k // 2] if k % 2 else even_ref.at[(mine ^ k) // 2]


def put_split(ref, cap, row):
    extra = ref.shape[0] - cap
    high = row.astype(BF16).astype(F32)
    down = iota((extra, row.shape[1]), 0)
    both = jnp.where(down == 0, high, jnp.where(down == 1, row - high, 0.0))
    ref[cap:, :] = jnp.zeros((extra, ref.shape[1]), BF16)
    ref[cap:, 0 : row.shape[1]] = both.astype(BF16)


def take_split(ref, cap, lanes):
    both = ref[cap:, 0:lanes].astype(F32)
    return both[0:1, :] + both[1:2, :]


def gelu_parts(pre):
    root = 0.7978845608028654
    cubic = 0.044715
    square = pre * pre
    upper = 0.5 + 0.5 * jnp.tanh(pre * (root + (root * cubic) * square))
    act = pre * upper
    return act, upper + act * (1.0 - upper) * (2.0 * root + (6.0 * root * cubic) * square)


class Copies:
    def __init__(self, sems):
        self.sems, self.count, self.open = sems, 0, []

    def start(self, source, target, kept=True):
        copy = pltpu.make_async_copy(source, target, self.sems.at[self.count])
        self.count += 1
        copy.start()
        if kept:
            self.open.append(copy)
        return copy

    def finish(self):
        for copy in self.open:
            copy.wait()


def expert_kernel(cfg, odd, me_ref, *refs):
    h, cap, n = cfg.hidden, cfg.cap, cfg.experts // 2
    many = n if odd else 1
    cot_ref, refs = refs[0], refs[1:]
    row_refs, refs = refs[:many], refs[many:]
    in_refs, out_refs, refs = refs[:h], refs[h : 2 * h], refs[2 * h :]
    if odd:
        before_ref, refs = refs[0], refs[1:]
    result_ref, back_refs, refs = refs[0], refs[1 : 1 + many], refs[1 + many :]
    pairs_ref, refs = refs[0], refs[1:]
    rows_all, cot_all, pairs_all, result_all, back_all, before_all, extra_in, extra_out = refs[:8]
    result_sum, back_sum, weights_all, in_sems, out_sems = refs[8:]
    total, width = rows_all.shape
    extra = extra_in.shape[1]
    mine = me_ref[0] // h
    loads, stores = Copies(in_sems), Copies(out_sems)
    ks = list(range(odd, 2 * n, 2))
    tiles = 2
    per = n // tiles
    tile = per * cap
    row_loads, weight_loads = [], []

    def load_rows(m):
        for i in range(m * per, (m + 1) * per):
            span = slice(i * cap, (i + 1) * cap)
            source = (mine ^ ks[i]) // 2
            row_ref = pick_ref(mine, ks[i], row_refs[0], row_refs)
            from_ref = cot_ref.at[source] if odd else cot_ref.at[source, mine % 2]
            row_loads.append(
                (
                    loads.start(row_ref.at[0:cap], rows_all.at[span], False),
                    loads.start(row_ref.at[cap : cap + extra], extra_in.at[i], False),
                    loads.start(from_ref, cot_all.at[span], False),
                )
            )

    load_rows(0)
    for i, ref in enumerate(in_turn(in_refs, out_refs)):
        held = weights_all.at[i, : ref.shape[0], : ref.shape[1]]
        weight_loads.append(loads.start(ref, held, False))
    for m in range(1, tiles):
        load_rows(m)
    if odd:
        before_loads = [loads.start(before_ref.at[i], before_all.at[i], False) for i in range(n)]
    gate_lanes = round_up(cap, LANES)
    eye = iota((cap, gate_lanes), 0) == iota((cap, gate_lanes), 1)
    units = in_refs[0].shape[1]
    gates = {}
    for m in range(tiles):
        span = slice(m * tile, (m + 1) * tile)
        for i in range(m * per, (m + 1) * per):
            for copy in row_loads[i]:
                copy.wait()
            rows = slice(i * cap, (i + 1) * cap)
            gates[i] = lane_sum(jnp.where(eye, take_split(extra_in.at[i], 0, gate_lanes), 0.0))
            pairs_all[rows, :] = (gates[i] * cot_all[rows, :].astype(F32)).astype(BF16)
        stores.start(pairs_all.at[span], pairs_ref.at[span])
        for b in range(h):
            if m == 0:
                weight_loads[2 * b].wait()
                weight_loads[2 * b + 1].wait()
            w_in, w_out = weights_all.at[2 * b, :, :units], weights_all.at[2 * b + 1, :units, :]
            act, slope = gelu_parts(mm(rows_all[span, :], w_in[...]))
            act_low = act.astype(BF16)
            act_grad = contract_last(pairs_all[span, :], w_out[...])
            pre_grad = (act_grad * slope).astype(BF16)
            result = mm(act_low, w_out[...])
            back = contract_last(pre_grad, w_in[...])
            if b == 0:
                result_sum[...] = result
                back_sum[...] = back
            elif b < h - 1:
                result_sum[...] += result
                back_sum[...] += back
            else:
                result_sum[...] += result
                back_all[span, :] = (back_sum[...] + back).astype(BF16)
        if odd and m == 0:
            for i in range(n):
                before_loads[i].wait()
                stores.start(before_all.at[i], result_ref.at[mine ^ (2 * i)])
        for i in range(m * per, (m + 1) * per):
            rows, k = slice(i * cap, (i + 1) * cap), ks[i]
            back_ref = pick_ref(mine, k, back_refs[0], back_refs)
            stores.start(back_all.at[rows], back_ref.at[0:cap])
            result = result_sum[(i - m * per) * cap : (i - m * per + 1) * cap, :]
            result_all[rows, :] = (gates[i] * result).astype(BF16)
            stores.start(result_all.at[rows], result_ref.at[mine ^ k if odd else i])
            dots = lane_sum(cot_all[rows, :].astype(F32) * result)
            put_split(extra_out.at[i], 0, row_sum(jnp.where(eye, dots, 0.0)))
            stores.start(extra_out.at[i], back_ref.at[cap : cap + extra])
    stores.finish()


def expert_part(cfg, odd, me, cot, rows, weights, before):
    n, h, cap, extra = cfg.experts // 2, cfg.hidden, cfg.cap, 16
    width, units = cot.shape[-1], weights[0].shape[1]
    slots = n * cap
    many = len(rows)
    side = max(width, units)
    args = [me, cot] + rows + weights + before
    outs = (
        [shape((2 * n if odd else n, cap, width), BF16)]
        + [shape(r.shape, BF16) for r in rows]
        + [shape((slots, width), BF16)]
    )
    outs = call(
        functools.partial(expert_kernel, cfg, odd),
        outs,
        [pltpu.VMEM((slots, width), BF16)] * 5
        + [pltpu.VMEM((n, cap, width), BF16)]
        + [pltpu.VMEM((n, extra, width), BF16)] * 2
        + [pltpu.VMEM((slots // 2, width), F32)] * 2
        + [pltpu.VMEM((2 * h, side, side), BF16)]
        + [pltpu.SemaphoreType.DMA((4 * n + 2 * h,)), pltpu.SemaphoreType.DMA((4 * n + 2,))],
        args,
        8 * slots * width * units * h,
        smem=(0,),
        far_in=range(1, len(args)),
        far_out=range(len(outs)),
    )
    return outs[0], outs[1 : 1 + many], outs[1 + many]


def weight_kernel(cfg, parts, me_ref, *refs):
    n, cap = cfg.experts, cfg.cap
    even_ref, odd_refs, refs = refs[0], refs[1 : 1 + n // 2], refs[1 + n // 2 :]
    pair_refs, in_refs, out_refs, refs = refs[:2], refs[2 : 2 + parts], refs[2 + parts : 2 + 2 * parts], refs[2 + 2 * parts :]
    grad_refs, refs = refs[:parts], refs[parts:]
    grads_all, refs = refs[:parts], refs[parts:]
    rows_all, pairs_all, rows_turned, pairs_turned, act_all, pre_all, weights_all, in_sems, out_sems = refs
    total, width = rows_all.shape
    half = total // 2
    units = act_all.shape[1]
    mine = me_ref[0] // cfg.hidden
    loads, stores = Copies(in_sems), Copies(out_sems)
    waits = {0: [], 1: []}
    weight_loads = []
    for odd in (0, 1):
        for i in range(n // 2):
            k = 2 * i + odd
            span = slice(odd * half + i * cap, odd * half + (i + 1) * cap)
            row_ref = pick_ref(mine, k, even_ref, odd_refs)
            waits[odd].append(loads.start(row_ref.at[0:cap], rows_all.at[span], False))
        span = slice(odd * half, (odd + 1) * half)
        waits[odd].append(loads.start(pair_refs[odd], pairs_all.at[span], False))
        if not odd:
            for i, ref in enumerate(in_turn(in_refs, out_refs)):
                held = weights_all.at[i, : ref.shape[0], : ref.shape[1]]
                weight_loads.append(loads.start(ref, held, False))
    tile = half // 2
    for p in range(parts):
        weight_loads[2 * p].wait()
        weight_loads[2 * p + 1].wait()
        w_in, w_out = weights_all.at[2 * p, :, :units], weights_all.at[2 * p + 1, :units, :]
        for m in range(4):
            if p == 0 and m % 2 == 0:
                for copy in waits[m // 2]:
                    copy.wait()
                span = slice(m // 2 * half, (m // 2 + 1) * half)
                rows_turned[:, span] = jnp.transpose(rows_all[span, :])
                pairs_turned[:, span] = jnp.transpose(pairs_all[span, :])
            span = slice(m * tile, (m + 1) * tile)
            act, slope = gelu_parts(mm(rows_all[span, :], w_in[...]))
            act_all[span, :] = act.astype(BF16)
            act_grad = contract_last(pairs_all[span, :], w_out[...])
            pre_all[span, :] = (act_grad * slope).astype(BF16)
        kept = grads_all[p]
        kept[:width, :] = mm(rows_turned[...], pre_all[...]).astype(kept.dtype)
        kept[width:, :] = mm(pairs_turned[...], act_all[...]).astype(kept.dtype)
        stores.start(kept, grad_refs[p])
    stores.finish()


def weight_part(cfg, picked, me, even_rows, odd_rows, pairs, ins, outs):
    width, units = ins[0].shape
    slots, parts = cfg.experts * cfg.cap, len(picked)
    args = [me, even_rows] + odd_rows + pairs + [ins[b] for b in picked] + [outs[b] for b in picked]
    kinds = [BF16 if b else F32 for b in picked]
    side = max(width, units)
    return call(
        functools.partial(weight_kernel, cfg, parts),
        [shape((2 * width, units), kind) for kind in kinds],
        [pltpu.VMEM((2 * width, units), kind) for kind in kinds]
        + [pltpu.VMEM((slots, width), BF16)] * 2
        + [pltpu.VMEM((width, slots), BF16)] * 2
        + [pltpu.VMEM((slots, units), BF16)] * 2
        + [pltpu.VMEM((2 * parts, side, side), BF16)]
        + [pltpu.SemaphoreType.DMA((cfg.experts + 2 + 2 * parts,)), pltpu.SemaphoreType.DMA((parts,))],
        args,
        8 * slots * width * units * parts,
        smem=(0,),
        far_in=range(1, len(args)),
        far_out=range(parts),
    )


def turn_add_kernel(*refs):
    terms, (sum_in, sum_out) = refs[:-2], refs[-2:]
    width = sum_in.shape[0]
    total = terms[0][...]
    for ref in terms[1:]:
        total = total + ref[...].astype(F32)
    sum_in[...] = total[:width, :]
    sum_out[...] = jnp.transpose(total[width:, :])


def rows_to_lanes(first, second, lane):
    down = iota((LANES, first.shape[1]), 0)
    return jnp.transpose(jnp.where(down == lane, first, jnp.where(down == lane + 1, second, 0.0)))


def backward_kernel(cfg, me_ref, side_ref, rows_ref, gates_ref, lse_ref, *refs):
    n, cap = cfg.experts, cfg.cap
    even_ref, odd_refs, refs = refs[0], refs[1 : 1 + n // 2], refs[1 + n // 2 :]
    hidden_in, cot_in, heads_in, tokens_in, proj_in, full_in, refs = *refs[:6], refs[6:]
    grad_ref, dense_outs, refs = refs[0], refs[1 : 1 + cfg.dense_outs], refs[1 + cfg.dense_outs :]
    back_all, extra_all, hidden_ref, cot_ref, heads_ref, tokens_ref, proj_ref, full_ref = refs[:8]
    routed_sum, routed_ref, logits_ref, low_ref, heads_grad_ref, bias_ref, qkv_ref = refs[8:15]
    turned_ref, dense_ref, grad_all, in_sems, out_sems = refs[15:]
    count, width = hidden_ref.shape
    extra = extra_all.shape[1]
    me = me_ref[0]
    mine = me // cfg.hidden
    loads, stores = Copies(in_sems), Copies(out_sems)
    back_loads = []
    for k in range(n):
        ref = pick_ref(mine, k, even_ref, odd_refs)
        span = slice(k * cap, (k + 1) * cap)
        back_loads.append(loads.start(ref.at[0:cap], back_all.at[span], False))
        back_loads.append(loads.start(ref.at[cap : cap + extra], extra_all.at[k], False))
    hidden_load = loads.start(hidden_in, hidden_ref, False)
    right = slice(3 * width, full_ref.shape[1])
    left = slice(0, 3 * width)
    right_load = loads.start(full_in.at[:, right], full_ref.at[:, right], False)
    cot_load = loads.start(cot_in, cot_ref, False)
    heads_load = loads.start(heads_in, heads_ref, False)
    proj_load = loads.start(proj_in, proj_ref, False)
    tokens_load = loads.start(tokens_in, tokens_ref, False)
    left_load = loads.start(full_in.at[:, left], full_ref.at[:, left], False)

    def relative(at):
        expert = side_ref[:, 5 + at : 6 + at]
        turned = (expert.astype(jnp.int32) ^ mine).astype(F32)
        return side_ref[:, at : at + 1] + (turned - expert) * cap

    one, two = relative(0), relative(1)
    slot = iota_f((count, n * cap), 1)
    pick = jnp.where((slot == one) | (slot == two), 1.0, 0.0).astype(BF16)
    chunk = 512
    for c in range(count // chunk):
        span = slice(c * chunk, (c + 1) * chunk)
        bias_ref[span, :] = jnp.where(side_ref[span, 4:5] == rows_ref[4:5, :], 0.0, NEG_FILL)
    for copy in back_loads:
        copy.wait()
    routed_sum[...] = mm(pick, back_all[...])
    gate_lanes = round_up(cap, LANES)
    dots_one = jnp.zeros((count, gate_lanes), F32)
    dots_two = jnp.zeros((count, gate_lanes), F32)
    lane_at = iota_f((count, gate_lanes), 1)
    for k in range(n):
        slot = jnp.where(lane_at < cap, lane_at + float(k * cap), -1.0)
        dots = take_split(extra_all.at[k], 0, gate_lanes)
        dots_one = dots_one + jnp.where(slot == one, dots, 0.0)
        dots_two = dots_two + jnp.where(slot == two, dots, 0.0)
    dot_one, dot_two = lane_sum(dots_one), lane_sum(dots_two)
    gate_one, gate_two = gates_ref[:, 0:1], gates_ref[:, 1:2]
    shared = gate_one * dot_one + gate_two * dot_two
    chosen_one = gate_one * (dot_one - shared)
    chosen_two = gate_two * (dot_two - shared)
    hidden_load.wait()
    right_load.wait()
    cot_load.wait()
    gain_one, bias_one, gain_two, bias_two = gain_rows(full_ref, 4 * width, cfg.gate_columns)
    gain_sum = jnp.zeros((1, width), F32)
    bias_sum = jnp.zeros((1, width), F32)
    for c in range(count // chunk):
        span = slice(c * chunk, (c + 1) * chunk)
        column = iota_f((chunk, cfg.gate_lanes), 1)
        logits = jnp.where(column == side_ref[span, 2:3], chosen_one[span], 0.0) + jnp.where(
            column == side_ref[span, 3:4], chosen_two[span], 0.0
        )
        logits = logits.astype(BF16)
        logits_ref[span, :] = logits
        routed_grad = routed_sum[span, :] + contract_last(logits, full_ref[:, 4 * width :])
        unit, inverse = norm_parts(hidden_ref[span, :])
        routed_ref[span, :] = (unit * gain_two + bias_two).astype(BF16)
        gain_sum = gain_sum + row_sum(routed_grad * unit)
        bias_sum = bias_sum + row_sum(routed_grad)
        hidden_grad = cot_ref[span, :].astype(F32) + norm_back(unit, inverse, gain_two, routed_grad)
        routed_sum[span, :] = hidden_grad
        low = hidden_grad.astype(BF16)
        low_ref[span, :] = low
        heads_grad_ref[span, :] = contract_last(low, full_ref[:, 3 * width : 4 * width]).astype(BF16)
    heads_load.wait()
    kind = dense_ref.dtype
    dense_ref[:, 3 * width : 4 * width] = contract_first(heads_ref[...], low_ref[...]).astype(kind)
    dense_ref[:, 4 * width :] = contract_first(routed_ref[...], logits_ref[...]).astype(kind)
    tile = 4 * width + cfg.gate_columns // LANES * LANES
    lane = cfg.gate_columns % LANES
    tile = slice(tile, tile + LANES)
    dense_ref[:, tile] += rows_to_lanes(gain_sum, bias_sum, lane + 2).astype(kind)
    proj_load.wait()
    lane_row = iota((1, LANES), 1)
    scale = HEAD_DIM ** (-0.5)
    block = 256

    def slab(i, carry):
        off = pl.multiple_of(i * LANES, LANES)
        queries = proj_ref[:, pl.ds(off, LANES)] * jnp.asarray(scale, BF16)
        keys = proj_ref[:, pl.ds(width + off, LANES)]
        values = proj_ref[:, pl.ds(2 * width + off, LANES)]
        grads = heads_grad_ref[:, pl.ds(off, LANES)]
        query_grad = [jnp.zeros((block, LANES), F32)] * (count // block)
        key_grad = jnp.zeros((count, LANES), F32)
        value_grad = jnp.zeros((count, LANES), F32)
        for half in (0, 1):
            part = jnp.where(lane_row // HEAD_DIM == half, 1.0, 0.0).astype(BF16)
            query_half, key_half, grads_half = queries * part, keys * part, grads * part
            logs = lse_ref[pl.ds(2 * i + half, 1), :]
            for q in range(count // block):
                span = slice(q * block, (q + 1) * block)
                scores = contract_last(key_half, queries[span]) + bias_ref[:, span] - logs[:, span]
                probs = jnp.exp(scores)
                prob_grad = contract_last(values, grads_half[span])
                score_grad = (probs * (prob_grad - row_sum(probs * prob_grad))).astype(BF16)
                value_grad = value_grad + mm(probs.astype(BF16), grads_half[span])
                key_grad = key_grad + mm(score_grad, query_half[span])
                query_grad[q] = query_grad[q] + contract_first(score_grad, key_half)
        for q in range(count // block):
            qkv_ref[q * block : (q + 1) * block, pl.ds(off, LANES)] = (query_grad[q] * scale).astype(BF16)
        qkv_ref[:, pl.ds(width + off, LANES)] = key_grad.astype(BF16)
        qkv_ref[:, pl.ds(2 * width + off, LANES)] = value_grad.astype(BF16)
        return carry

    lax.fori_loop(0, width // LANES, slab, 0)
    tokens_load.wait()
    left_load.wait()
    gain_sum = jnp.zeros((1, width), F32)
    bias_sum = jnp.zeros((1, width), F32)
    for c in range(count // chunk):
        span = slice(c * chunk, (c + 1) * chunk)
        normed_grad = contract_last(qkv_ref[span, :], full_ref[:, left])
        unit, inverse = norm_parts(tokens_ref[span, :].astype(F32))
        low_ref[span, :] = (unit * gain_one + bias_one).astype(BF16)
        gain_sum = gain_sum + row_sum(normed_grad * unit)
        bias_sum = bias_sum + row_sum(normed_grad)
        grad_all[span, :] = routed_sum[span, :] + norm_back(unit, inverse, gain_one, normed_grad)
        stores.start(grad_all.at[span], grad_ref.at[span])
    turned_ref[...] = jnp.transpose(low_ref[...])
    dense_ref[:, tile] += rows_to_lanes(gain_sum, bias_sum, lane).astype(kind)
    owners = [mask for masks in cfg.owners for mask in masks]
    rows = width // len(owners)
    for c in range(width // chunk):
        span = slice(c * chunk, (c + 1) * chunk)
        dense_ref[span, left] = mm(turned_ref[span, :], qkv_ref[...]).astype(kind)
    if len(dense_outs) == 1:
        stores.start(dense_ref, dense_outs[0])
    else:
        for at, mask in enumerate(owners):
            half = at * 2 // len(owners)
            to = (at - half * len(owners) // 2) * rows
            source = pl.multiple_of((me ^ mask) * rows, rows)
            stores.start(dense_ref.at[pl.ds(source, rows)], dense_outs[half].at[to : to + rows])
    stores.finish()


def output_kernel(cfg, side_ref, hidden_ref, result_ref, out_ref):
    count, width = hidden_ref.shape
    slot = iota_f((count, cfg.experts * cfg.cap), 1)
    pick = (slot == side_ref[:, 0:1]) | (slot == side_ref[:, 1:2])
    mixed = mm(jnp.where(pick, 1.0, 0.0).astype(BF16), result_ref[...])
    out_ref[...] = (hidden_ref[...] + mixed).astype(BF16)


class Config:
    pass


def after(value, other):
    return lax.optimization_barrier((value, other))[0]


def apart(always, part, *args):
    given = jax.eval_shape(part, *args)

    def never(*_):
        return jax.tree.map(lambda s: jnp.zeros(s.shape, s.dtype), given)

    return lax.cond(always, part, never, *args)


def swap_hidden(value, mask):
    size = lax.axis_size("hidden")
    return lax.ppermute(value, "hidden", [(i, i ^ mask) for i in range(size)])


def swap_expert(value, mask):
    size = lax.axis_size("expert")
    return lax.ppermute(value, "expert", [(i, i ^ mask) for i in range(size)])


def gather_rest(own):
    blocks = [own]
    bit = 2
    while bit < lax.axis_size("hidden"):
        blocks += [swap_hidden(block, bit) for block in blocks]
        bit *= 2
    return blocks


def gather_core(half):
    return [swap_hidden(block, 1) for block in half]


def in_turn(first, second):
    return [block for pair in zip(first, second) for block in pair]


def sum_rest(blocks):
    held = {i + 2: [b] for i, b in enumerate(blocks)}
    low = {i: v + [swap_hidden(held[i + 1][0], 1)] for i, v in held.items() if not i & 1}
    held = {0: [], **low}
    bit = 2
    while bit < len(blocks) + 2:
        low = {i: v for i, v in held.items() if not i & bit}
        for i in low:
            value = functools.reduce(jnp.add, held[i ^ bit])
            if 2 * bit == len(blocks) + 2:
                return low[0], value
            low[i] = low[i] + [swap_hidden(value, bit)]
        held = low
        bit *= 2


def body(
    tokens,
    lengths,
    task_ids,
    routes,
    w_qkv,
    w_attn_out,
    w_gate,
    ln1_gain,
    ln1_bias,
    ln2_gain,
    ln2_bias,
    w_in,
    w_out,
    cotangent,
):
    count, width = tokens.shape
    cfg = Config()
    cfg.experts = lax.axis_size("expert")
    cfg.hidden = lax.axis_size("hidden")
    experts, hidden = cfg.experts, cfg.hidden
    cfg.cap = cap = (3 * count * routes.shape[1] + 2 * experts - 1) // (2 * experts)
    cfg.gate_columns = w_gate.shape[1]
    cfg.gate_lanes = round_up(cfg.gate_columns + 4, LANES)
    devices = experts * hidden
    groups = Groups(devices)
    shard_rows = w_qkv.shape[0]
    staged = shard_rows % 16 == 0
    cfg.owners = groups.owners()
    me = (lax.axis_index("expert") * hidden + lax.axis_index("hidden")).astype(jnp.int32)[None]
    extra = 16
    units = w_in.shape[2]
    slots = experts * cap
    wide = 4 * width + cfg.gate_lanes
    one_dot = 2 * count * width * width

    packed = call(
        pack_kernel,
        shape((shard_rows, wide), BF16),
        [],
        [w_qkv, w_attn_out, w_gate]
        + [v.reshape(1, shard_rows) for v in (ln1_gain, ln1_bias, ln2_gain, ln2_bias)],
        1,
    )
    always = lengths[0, 0] > 0

    def first_part(packed, lengths, task_ids, routes, cotangent):
        far = groups.gather_far(packed) if staged else packed
        made = call(
            functools.partial(prep_kernel, cfg),
            [
                shape((count, LANES), F32),
                shape((8, count), F32),
                shape((experts // 2, 2, cap, width), BF16),
            ],
            [
                pltpu.VMEM((count, width), BF16),
                pltpu.VMEM((count, LANES), F32),
                pltpu.VMEM((8, count), F32),
                pltpu.VMEM((experts // 2, 2, cap, width), BF16),
                pltpu.SemaphoreType.DMA((1,)),
                pltpu.SemaphoreType.DMA((2 + experts,)),
            ],
            [lengths, task_ids, routes, cotangent],
            3 * one_dot,
            far_in=(3,),
            far_out=(0, 1, 2),
        )
        return far, made

    dense_far, (side, rows, sent_cot) = apart(
        always, first_part, packed, lengths, task_ids, routes.T, cotangent
    )
    if staged:
        dense_blocks = groups.gather_near(dense_far)
        reached = dense_blocks[1 : len(groups.mid)]
    else:
        dense_blocks = [lax.all_gather(packed, BOTH, axis=0, tiled=True)]
        reached = dense_blocks[0]
    cfg.blocks = len(dense_blocks)
    parity = [list(range(i, experts, 2)) for i in (0, 1)]

    def exchange_even(value):
        return lax.all_to_all(
            value, "expert", split_axis=0, concat_axis=0, axis_index_groups=parity, tiled=True
        )

    def exchange_odd(values):
        return [swap_expert(value, 2 * i + 1) for i, value in enumerate(values)]

    cot_even = exchange_even(sent_cot)
    other = 1 - lax.axis_index("expert") % 2
    cot_odd = lax.dynamic_index_in_dim(cot_even, other, 1, keepdims=False)
    in_half = gather_rest(after(w_in[0], reached))

    outs = call(
        functools.partial(forward_kernel, cfg),
        [
            shape((width, wide), BF16),
            shape((count, 3 * width), BF16),
            shape((count, width), BF16),
            shape((HEADS, count), F32),
            shape((count, width), F32),
            shape((count, LANES), F32),
        ]
        + [shape((experts // 2, cap + extra, width), BF16)]
        + [shape((cap + extra, width), BF16)] * (experts // 2),
        [
            pltpu.VMEM((width, wide), BF16),
            pltpu.VMEM((count, 3 * width), BF16),
            pltpu.VMEM((count, width), BF16),
            pltpu.VMEM((HEADS, count), F32),
            pltpu.VMEM((count, width), F32),
            pltpu.VMEM((count, LANES), F32),
            pltpu.VMEM((experts, extra, width), BF16),
            pltpu.VMEM((slots, width), BF16),
            pltpu.VMEM((slots, count), BF16),
            pltpu.VMEM((count, count), F32),
            pltpu.VMEM((count, width), BF16),
            pltpu.VMEM((count, LANES), F32),
            pltpu.SemaphoreType.DMA((devices,)),
            pltpu.SemaphoreType.DMA((6 + 2 * experts,)),
        ],
        [me, side, rows, tokens] + dense_blocks,
        12 * one_dot,
        smem=(0,),
        far_in=range(4, 4 + cfg.blocks),
        far_out=range(7 + experts // 2),
    )
    full, proj, heads, lse, hidden_one, gates = outs[:6]
    send_rows = outs[6:]
    def even_part(even_send, odd_send, cot_even, cot_odd, in_half, own_out):
        out_half = gather_rest(own_out)
        more_in, more_out = gather_core(in_half), gather_core(out_half)
        blocks = in_turn(in_half, more_in) + in_turn(out_half, more_out)
        even_rows = exchange_even(even_send)
        odd_rows = exchange_odd(odd_send)
        cot_odd = swap_expert(cot_odd, 1)
        out = expert_part(cfg, 0, me, cot_even, [even_rows], blocks, [])
        return even_rows, odd_rows, cot_odd, more_in, out_half[1:], more_out, out

    def odd_part(even_send, even_rows, odd_rows, cot_odd, in_blocks, out_blocks, before, even_pairs):
        even_back = exchange_even(even_send)
        blocks = in_blocks + out_blocks
        result, sends, pairs = expert_part(cfg, 1, me, cot_odd, odd_rows, blocks, [before])
        odd_back = exchange_odd(sends)
        sums = apart(always, far_weights, even_rows, odd_rows, [even_pairs, pairs], in_blocks, out_blocks)
        return [even_back] + odd_back, result, pairs, *sums

    def far_weights(even_rows, odd_rows, pairs, in_blocks, out_blocks):
        picked = [b for b in range(hidden) if b > 1]
        return sum_rest(
            weight_part(cfg, picked, me, even_rows, odd_rows, pairs, in_blocks, out_blocks)
        )

    def own_weights(even_rows, odd_rows, pairs, in_blocks, out_blocks):
        return weight_part(cfg, [0, 1], me, even_rows, odd_rows, pairs, in_blocks, out_blocks)

    even_rows, odd_rows, cot_odd, more_in, rest_out, more_out, even_out = apart(
        always, even_part, send_rows[0], send_rows[1:], cot_even, cot_odd, in_half, w_out[0]
    )
    out_half = [w_out[0]] + rest_out
    in_blocks, out_blocks = in_turn(in_half, more_in), in_turn(out_half, more_out)
    back, result, odd_pairs, held, value = apart(
        always,
        odd_part,
        even_out[1][0],
        even_rows,
        odd_rows,
        cot_odd,
        in_blocks,
        out_blocks,
        even_out[0],
        even_out[2],
    )
    pairs = [even_out[2], odd_pairs]
    returned = lax.all_to_all(
        after(result, back), "expert", split_axis=0, concat_axis=0, tiled=True
    )
    if staged:
        dense_shapes = [shape((width // 2, wide), BF16)] * 2
    else:
        dense_shapes = [shape((width, wide), F32)]
    cfg.dense_outs = len(dense_shapes)

    def back_part(value, back):
        args = [me, side, rows, gates, lse] + back + [hidden_one, cotangent, heads, tokens, proj, full]
        outs = call(
            functools.partial(backward_kernel, cfg),
            [shape((count, width), F32)] + dense_shapes,
            [
                pltpu.VMEM((slots, width), BF16),
                pltpu.VMEM((experts, extra, width), BF16),
                pltpu.VMEM((count, width), F32),
                pltpu.VMEM((count, width), BF16),
                pltpu.VMEM((count, width), BF16),
                pltpu.VMEM((count, width), BF16),
                pltpu.VMEM((count, 3 * width), BF16),
                pltpu.VMEM((width, wide), BF16),
                pltpu.VMEM((count, width), F32),
                pltpu.VMEM((count, width), BF16),
                pltpu.VMEM((count, cfg.gate_lanes), BF16),
                pltpu.VMEM((count, width), BF16),
                pltpu.VMEM((count, width), BF16),
                pltpu.VMEM((count, count), F32),
                pltpu.VMEM((count, 3 * width), BF16),
                pltpu.VMEM((width, count), BF16),
                pltpu.VMEM((width, wide), dense_shapes[0].dtype),
                pltpu.VMEM((count, width), F32),
                pltpu.SemaphoreType.DMA((2 * experts + 7,)),
                pltpu.SemaphoreType.DMA((4 + devices,)),
            ],
            args,
            19 * one_dot,
            smem=(0,),
            far_in=range(5, len(args)),
            far_out=range(1 + len(dense_shapes)),
        )
        return swap_hidden(value, hidden // 2), outs

    last, outs = apart(always, back_part, value, back)
    reached = held + [last]
    grad_tokens = outs[0]

    def last_weights(blocks):
        got = [groups.swap(b, m) for b, m in zip(blocks[1:], groups.mid[1:])]
        return got, own_weights(even_rows, odd_rows, pairs, in_blocks, out_blocks)

    def last_sums(blocks, own, more, reached, returned):
        layer_out = call(
            functools.partial(output_kernel, cfg),
            shape((count, width), BF16),
            [],
            [side, hidden_one, returned.reshape(slots, width)],
            6 * one_dot,
        )
        got = [groups.swap(b, m) for b, m in zip(blocks[1:], groups.far[1:])]
        terms = [own, swap_hidden(more, 1)] + reached
        grad_in, grad_out = call(
            turn_add_kernel,
            [shape((width, units), F32), shape((units, width), F32)],
            [],
            terms,
            4 * width * units,
            limit=2 * SMALL_LIMIT,
        )
        return got, grad_in, grad_out, layer_out

    blocks = [None]
    if staged:
        blocks = add_parts(outs[1], [groups.swap(outs[2], 1)], len(groups.mid))
    got, (own, more) = apart(always, last_weights, blocks)
    if staged:
        blocks = add_parts(blocks[0], got, len(groups.far))
    got, grad_in, grad_out, layer_out = apart(
        always, last_sums, blocks, own, more, reached, returned
    )
    if staged:
        dense_terms = blocks[:1] + got
    else:
        dense_terms = [lax.psum_scatter(outs[1], BOTH, scatter_dimension=0, tiled=True)]
    dense_outs = call(
        functools.partial(split_kernel, cfg),
        [shape((shard_rows, c), F32) for c in (3 * width, width, cfg.gate_columns)]
        + [shape((1, shard_rows), F32)] * 4,
        [],
        dense_terms,
        shard_rows * wide,
        limit=SMALL_LIMIT,
    )

    return (
        layer_out,
        grad_tokens,
        *dense_outs[:3],
        *[v.reshape(shard_rows) for v in dense_outs[3:]],
        grad_in[None],
        grad_out[None],
    )


def solution(mesh):
    split = P(BOTH, None)
    vector = P(BOTH)
    placed = (split,) * 7 + (vector,) * 4 + (P("expert", None, "hidden"), P("expert", "hidden", None), split)
    return jax.shard_map(
        body,
        mesh=mesh,
        in_specs=placed,
        out_specs=(split,) * 5
        + (vector,) * 4
        + (P("expert", None, "hidden"), P("expert", "hidden", None)),
        check_vma=False,
    )
```

profile of v0, /device:TPU:0, one launch (start us, length us, event | category | flops | bytes accessed | tf_op | source)
XLA Modules:
  0.0 204.7 jit_solution(8532437356126737149)
XLA Ops:
  2.2 11.3 %conditional.7 = (bf16[64,2304]{1,0:T(8,128)(2,1)S(1)}, f32[512,128]{1,0:T(8,128)S(1)}, f32[8,512]{1,0:T(8,128)S(1)}, bf16[4,2,192,512]{3,2,1,0:T(8,128)(2,1)}) conditional(s32[]{:T(128)} %convert_element_type.5, () %tuple.75, (bf16[16,2304]{1,0:T(8,128)(2,1)S(1)}, s32[1,16]{1,0:T(1,128)}, s32[1,16]{1,0:T(1,128)}, s32[2,512]{1,0:T(2,128)}, ...), branch_computations={%region_0.0_spmd, %region_1.0_spmd} | conditional | flops 1179649 | bytes 2146348 | solution.py:787
  2.2 5.1 %collective-permute-start.15 = (bf16[16,2304]{1,0:T(8,128)(2,1)S(1)}, bf16[16,2304]{1,0:T(8,128)(2,1)S(1)}, u32[]{:S(2)}, u32[]{:S(2)}) collective-permute-start(bf16[16,2304]{1,0:T(8,128)(2,1)S(1)} %get-tuple-element.210), channel_id=1, source_target_pairs={{0,24},{1,25},{2,26},{3,27},{4,28},{5,29},{6,30},{7,31},{8,16},{9,... | collective-permute-start | bytes 221192 | tf_op jit(solution)/shard_map/cond/branch_1_fun/ppermute | solution.py:191
  8.0 4.1 %branch_1_fun.8 = (f32[512,128]{1,0:T(8,128)S(1)}, f32[8,512]{1,0:T(8,128)S(1)}, bf16[4,2,192,512]{3,2,1,0:T(8,128)(2,1)}) custom-call(s32[1,16]{1,0:T(1,128)} %get-tuple-element.211.lens_ref, s32[1,16]{1,0:T(1,128)} %get-tuple-element.470.tasks_ref, s32[2,512]{1,0:T(2,128)} %get-tuple-element.213.routes_ref, bf16[512,512]{1,0:T(8,128)(2,1)} %get-tuple-element.214.cot_in), custom_call_target="tpu_custom_call" | custom-call | flops 1 | bytes 1 | tf_op jit(solution)/shard_map/cond/branch_1_fun/pallas_call | solution.py:80
  12.1 1.5 collective-permute-done.14
  13.6 4.3 %all-to-all-start.2 = ((bf16[4,2,192,512]{3,2,1,0:T(8,128)(2,1)}), bf16[4,2,192,512]{3,2,1,0:T(8,128)(2,1)S(1)}, u32[]{:S(2)}, u32[]{:S(2)}) async-start(bf16[4,2,192,512]{3,2,1,0:T(8,128)(2,1)} %get-tuple-element.408), calls=%async_computation.2 | async-start | bytes 3145728 | tf_op jit(solution)/shard_map/all_to_all | solution.py:916
  17.9 2.5 %collective-permute-start.28 = (bf16[64,2304]{1,0:T(8,128)(2,1)S(1)}, bf16[64,2304]{1,0:T(8,128)(2,1)}, u32[]{:S(2)}, u32[]{:S(2)}) collective-permute-start(bf16[64,2304]{1,0:T(8,128)(2,1)S(1)} %get-tuple-element.402.refs_0_), channel_id=1, source_target_pairs={{0,6},{1,7},{2,4},{3,5},{4,2},{5,3},{6,0},{7,1},{8,14},{9,15},{10,... | collective-permute-start | bytes 884744 | tf_op jit(solution)/shard_map/ppermute | solution.py:191
  21.5 7.5 %collective-permute-done.28.refs_3_ = bf16[64,2304]{1,0:T(8,128)(2,1)} collective-permute-done((bf16[64,2304]{1,0:T(8,128)(2,1)S(1)}, bf16[64,2304]{1,0:T(8,128)(2,1)}, u32[]{:S(2)}, u32[]{:S(2)}) %collective-permute-start.28) | collective-permute-done | bytes 294944 | tf_op jit(solution)/shard_map/ppermute | solution.py:191
  29.0 4.6 %collective-permute-done.27.refs_2_ = bf16[64,2304]{1,0:T(8,128)(2,1)} collective-permute-done((bf16[64,2304]{1,0:T(8,128)(2,1)S(1)}, bf16[64,2304]{1,0:T(8,128)(2,1)}, u32[]{:S(2)}, u32[]{:S(2)}) %collective-permute-start.27) | collective-permute-done | bytes 294944 | tf_op jit(solution)/shard_map/ppermute | solution.py:191
  33.6 1.4 collective-permute-start.33
  38.2 14.0 %shard_map.223 = (bf16[512,2304]{1,0:T(8,128)(2,1)}, bf16[512,1536]{1,0:T(8,128)(2,1)}, bf16[512,512]{1,0:T(8,128)(2,1)}, f32[8,512]{1,0:T(8,128)}, f32[512,512]...) custom-call(s32[1]{0:T(128)} %bitcast.5.me_ref, ...), custom_call_target="tpu_custom_call" | custom-call | flops 1 | bytes 1 | tf_op jit(solution)/shard_map/pallas_call | solution.py:80
  52.2 2.1 %all-to-all-done.2 = bf16[4,2,192,512]{3,2,1,0:T(8,128)(2,1)S(1)} async-done(((bf16[4,2,192,512]{3,2,1,0:T(8,128)(2,1)}), bf16[4,2,192,512]{3,2,1,0:T(8,128)(2,1)S(1)}, u32[]{:S(2)}, u32[]{:S(2)}) %all-to-all-start.2) | async-done | bytes 1572896 | tf_op jit(solution)/shard_map/all_to_all | solution.py:916
  54.3 44.0 %conditional.8 = (bf16[4,208,512]{2,1,0:T(8,128)(2,1)}, bf16[208,512]{1,0:T(8,128)(2,1)}, bf16[208,512]{1,0:T(8,128)(2,1)}, bf16[208,512]{1,0:T(8,128)(2,1)}, bf...) conditional(s32[]{:T(128)} %convert_element_type.5, () %tuple.74, ...), branch_computations={%region_2.3_spmd, %region_3.4_spmd} | conditional | flops 16 | bytes 21168832 | solution.py:787
  54.3 4.2 %all-to-all-start.1 = ((bf16[4,208,512]{2,1,0:T(8,128)(2,1)}), bf16[4,208,512]{2,1,0:T(8,128)(2,1)}, u32[]{:S(2)}, u32[]{:S(2)}) async-start(bf16[4,208,512]{2,1,0:T(8,128)(2,1)} %get-tuple-element.218), calls=%async_computation.1 | async-start | bytes 1703936 | tf_op jit(solution)/shard_map/cond/branch_1_fun/all_to_all | solution.py:916
  58.5 1.8 collective-permute-start.23
  61.3 1.5 collective-permute-start.20
  63.3 8.3 %collective-permute-done.23.refs_8_ = bf16[512,512]{1,0:T(8,128)(2,1)} collective-permute-done((bf16[512,512]{1,0:T(8,128)(2,1)S(1)}, bf16[512,512]{1,0:T(8,128)(2,1)}, u32[]{:S(2)}, u32[]{:S(2)}) %collective-permute-start.23) | collective-permute-done | bytes 524320 | tf_op jit(solution)/shard_map/cond/branch_1_fun/ppermute | solution.py:792
  71.6 1.7 collective-permute-start.16
  73.3 1.4 collective-permute-start.17
  74.7 3.5 %collective-permute-start.18 = (bf16[208,512]{1,0:T(8,128)(2,1)}, bf16[208,512]{1,0:T(8,128)(2,1)}, u32[]{:S(2)}, u32[]{:S(2)}) collective-permute-start(bf16[208,512]{1,0:T(8,128)(2,1)} %get-tuple-element.221), channel_id=1, source_target_pairs={{0,20},{4,16},{8,28},{12,24},{16,4},{20,0},{24,12},{28,8},{1,21},{... | collective-permute-start | bytes 638984 | tf_op jit(solution)/shard_map/cond/branch_1_fun/ppermute | solution.py:797
  78.4 1.3 all-to-all-done.1.refs_1_
  79.7 11.4 %branch_1_fun.9 = (bf16[4,192,512]{2,1,0:T(8,128)(2,1)}, bf16[4,208,512]{2,1,0:T(8,128)(2,1)}, bf16[768,512]{1,0:T(8,128)(2,1)}) custom-call(s32[1]{0:T(128)} %get-tuple-element.229.me_ref, bf16[4,2,192,512]{3,2,1,0:T(8,128)(2,1)S(1)} %get-tuple-element.223.refs_0_, bf16[4,208,512]{2,1,0:T(8,128)(2,1)} %all-to-all-done.1.refs_1_, ...), custom_call_target="tpu_custom_call" | custom-call | flops 1 | bytes 1 | tf_op jit(solution)/shard_map/cond/branch_1_fun/pallas_call | solution.py:80
  91.1 6.9 %collective-permute-done.16 = bf16[208,512]{1,0:T(8,128)(2,1)} collective-permute-done((bf16[208,512]{1,0:T(8,128)(2,1)}, bf16[208,512]{1,0:T(8,128)(2,1)}, u32[]{:S(2)}, u32[]{:S(2)}) %collective-permute-start.16) | collective-permute-done | bytes 213024 | tf_op jit(solution)/shard_map/cond/branch_1_fun/ppermute | solution.py:797
  98.3 40.3 %conditional.9 = (bf16[4,208,512]{2,1,0:T(8,128)(2,1)}, bf16[208,512]{1,0:T(8,128)(2,1)}, bf16[208,512]{1,0:T(8,128)(2,1)}, bf16[208,512]{1,0:T(8,128)(2,1)}, bf...) conditional(s32[]{:T(128)} %convert_element_type.5, () %tuple.73, ...), branch_computations={%region_4.5_spmd, %region_5.8_spmd} | conditional | flops 524291 | bytes 13304215 | solution.py:787
  98.3 4.7 %all-to-all-start = ((bf16[4,208,512]{2,1,0:T(8,128)(2,1)}), bf16[4,208,512]{2,1,0:T(8,128)(2,1)}, u32[]{:S(2)}, u32[]{:S(2)}) async-start(bf16[4,208,512]{2,1,0:T(8,128)(2,1)} %get-tuple-element.247), calls=%async_computation | async-start | bytes 1703936 | tf_op jit(solution)/shard_map/cond/branch_1_fun/all_to_all | solution.py:916
  103.0 11.6 %branch_1_fun.11 = (bf16[8,192,512]{2,1,0:T(8,128)(2,1)}, bf16[208,512]{1,0:T(8,128)(2,1)}, bf16[208,512]{1,0:T(8,128)(2,1)}, bf16[208,512]{1,0:T(8,128)(2,1)}, ...) custom-call(s32[1]{0:T(128)} %get-tuple-element.248.me_ref, bf16[4,192,512]{2,1,0:T(8,128)(2,1)} %get-tuple-element.249.refs_0_, ...), custom_call_target="tpu_custom_call" | custom-call | flops 1 | bytes 1 | tf_op jit(solution)/shard_map/cond/branch_1_fun/pallas_call | solution.py:80
  114.7 1.5 collective-permute-start.1
  116.2 2.0 collective-permute-start.2
  118.2 3.3 %collective-permute-start.3 = (bf16[208,512]{1,0:T(8,128)(2,1)}, bf16[208,512]{1,0:T(8,128)(2,1)}, u32[]{:S(2)}, u32[]{:S(2)}) collective-permute-start(bf16[208,512]{1,0:T(8,128)(2,1)} %get-tuple-element.265), channel_id=1, source_target_pairs={{0,20},{4,16},{8,28},{12,24},{16,4},{20,0},{24,12},{28,8},{1,21},{... | collective-permute-start | bytes 638984 | tf_op jit(solution)/shard_map/cond/branch_1_fun/ppermute | solution.py:797
  121.5 16.4 %conditional = (bf16[1024,512]{1,0:T(8,128)(2,1)}) conditional(s32[]{:T(128)} %convert_element_type.0, () %tuple.46, (s32[1]{0:T(128)}, bf16[4,208,512]{2,1,0:T(8,128)(2,1)}, bf16[208,512]{1,0:T(8,128)(2,1)}, bf16[208,512]{1,0:T(8,128)(2,1)}, bf16[208,512]{1,0:T(8,128)(2,1)}, /*index=5*/bf16[208,512]{1,0:T(8,128)(2,1)}, bf16[768,512]{1,0:T(8,128)(2,1)}, ...), branch_computations={%region_6.6_spmd, %region_7.7_spmd} | conditional | flops 524289 | bytes 7340081 | solution.py:787
  121.9 10.6 %branch_1_fun.10 = (bf16[1024,512]{1,0:T(8,128)(2,1)}, bf16[1024,512]{1,0:T(8,128)(2,1)}) custom-call(s32[1]{0:T(128)} %get-tuple-element.233.me_ref, bf16[4,208,512]{2,1,0:T(8,128)(2,1)} %get-tuple-element.234.refs_0_, bf16[208,512]{1,0:T(8,128)(2,1)} %get-tuple-element.235.refs_1_, bf16[208,512]{1,0:T(8,128)(2,1)} %get-tuple-element.236.refs_2_, ...), custom_call_target="tpu_custom_call" | custom-call | flops 1 | bytes 1 | tf_op jit(solution)/shard_map/cond/branch_1_fun/cond/branch_1_fun/pallas_call | solution.py:80
  132.6 2.9 %collective-permute-done = bf16[1024,512]{1,0:T(8,128)(2,1)S(1)} collective-permute-done((bf16[1024,512]{1,0:T(8,128)(2,1)}, bf16[1024,512]{1,0:T(8,128)(2,1)S(1)}, u32[]{:S(2)}, u32[]{:S(2)}) %collective-permute-start) | collective-permute-done | bytes 1048608 | tf_op jit(solution)/shard_map/cond/branch_1_fun/cond/branch_1_fun/ppermute | solution.py:792
  135.5 2.5 %add.14 = bf16[1024,512]{1,0:T(8,128)(2,1)} add(bf16[1024,512]{1,0:T(8,128)(2,1)} %get-tuple-element.245, bf16[1024,512]{1,0:T(8,128)(2,1)S(1)} %collective-permute-done) | non-fusion elementwise | flops 524288 | bytes 3145728 | tf_op jit(solution)/shard_map/cond/branch_1_fun/cond/branch_1_fun/add | solution.py:825
  138.6 6.1 %all-to-all-start.3 = ((bf16[8,192,512]{2,1,0:T(8,128)(2,1)}), bf16[8,192,512]{2,1,0:T(8,128)(2,1)}, u32[]{:S(2)}, u32[]{:S(2)}) async-start(bf16[8,192,512]{2,1,0:T(8,128)(2,1)} %get-tuple-element.450), calls=%async_computation.3 | async-start | bytes 3145728 | tf_op jit(solution)/shard_map/all_to_all | solution.py:1009
  144.8 24.9 %conditional.10 = (bf16[1024,512]{1,0:T(8,128)(2,1)}, f32[512,512]{1,0:T(8,128)}, bf16[256,2304]{1,0:T(8,128)(2,1)S(1)}, bf16[256,2304]{1,0:T(8,128)(2,1)S(1)}) conditional(s32[]{:T(128)} %convert_element_type.5, () %tuple.72, (bf16[1024,512]{1,0:T(8,128)(2,1)}, s32[1]{0:T(128)}, f32[512,128]{1,0:T(8,128)S(1)}, f32[8,512]{1,0:T(8,128)S(1)}, ...), branch_computations={%region_8.9_spmd, %region_9.10_spmd} | conditional | flops 1 | bytes 4456490 | solution.py:787
  144.8 1.6 collective-permute-start.5
  146.4 21.3 %branch_1_fun.12 = (f32[512,512]{1,0:T(8,128)}, bf16[256,2304]{1,0:T(8,128)(2,1)S(1)}, bf16[256,2304]{1,0:T(8,128)(2,1)S(1)}) custom-call(s32[1]{0:T(128)} %get-tuple-element.273.me_ref, f32[512,128]{1,0:T(8,128)S(1)} %get-tuple-element.274.side_ref, f32[8,512]{1,0:T(8,128)S(1)} %get-tuple-element.275.rows_ref, f32[512,128]{1,0:T(8,128)} %get-tuple-element.276.gates_ref, ...), custom_call_target="tpu_custom_call" | custom-call | flops 1 | bytes 1 | tf_op jit(solution)/shard_map/cond/branch_1_fun/pallas_call | solution.py:80
  167.6 2.0 collective-permute-done.5
  169.7 2.8 %collective-permute-done.34.refs_0_ = bf16[256,2304]{1,0:T(8,128)(2,1)S(1)} collective-permute-done((bf16[256,2304]{1,0:T(8,128)(2,1)S(1)}, bf16[256,2304]{1,0:T(8,128)(2,1)S(1)}, u32[]{:S(2)}, u32[]{:S(2)}) %collective-permute-start.34) | collective-permute-done | bytes 1179680 | tf_op jit(solution)/shard_map/ppermute | solution.py:191
  172.8 17.0 %conditional.11 = (bf16[64,2304]{1,0:T(8,128)(2,1)}, bf16[64,2304]{1,0:T(8,128)(2,1)}, bf16[64,2304]{1,0:T(8,128)(2,1)}, f32[1024,512]{1,0:T(8,128)S(1)}, bf16[1024,512]{1,0:T(8,128)(2,1)}) conditional(s32[]{:T(128)} %convert_element_type.5, () %tuple.81, (bf16[64,2304]{1,0:T(8,128)(2,1)S(1)}, bf16[64,2304]{1,0:T(8,128)(2,1)S(1)}, ...), branch_computations={%region_10.11_spmd, %region_11.12_spmd} | conditional | flops 1 | bytes 5636285 | solution.py:787
  174.0 1.7 collective-permute-start.7
  176.6 11.4 %branch_1_fun.13 = (f32[1024,512]{1,0:T(8,128)S(1)}, bf16[1024,512]{1,0:T(8,128)(2,1)}) custom-call(s32[1]{0:T(128)} %get-tuple-element.295.me_ref, bf16[4,208,512]{2,1,0:T(8,128)(2,1)} %get-tuple-element.296.refs_0_, bf16[208,512]{1,0:T(8,128)(2,1)} %get-tuple-element.297.refs_1_, bf16[208,512]{1,0:T(8,128)(2,1)} %get-tuple-element.298.refs_2_, ...), custom_call_target="tpu_custom_call" | custom-call | flops 1 | bytes 1 | tf_op jit(solution)/shard_map/cond/branch_1_fun/pallas_call | solution.py:80
  188.0 1.8 collective-permute-done.8
  191.0 11.6 %conditional.12 = (bf16[16,2304]{1,0:T(8,128)(2,1)}, bf16[16,2304]{1,0:T(8,128)(2,1)}, bf16[16,2304]{1,0:T(8,128)(2,1)}, bf16[512,512]{1,0:T(8,128)(2,1)S(1)}, f...) conditional(s32[]{:T(128)} %convert_element_type.5, () %tuple.71, (bf16[16,2304]{1,0:T(8,128)(2,1)S(1)}, ...), branch_computations={%region_12.13_spmd, %region_13.14_spmd} | conditional | flops 2 | bytes 5079250 | solution.py:787
  191.1 2.7 %collective-permute-start.9 = (bf16[16,2304]{1,0:T(8,128)(2,1)S(1)}, bf16[16,2304]{1,0:T(8,128)(2,1)}, u32[]{:S(2)}, u32[]{:S(2)}) collective-permute-start(bf16[16,2304]{1,0:T(8,128)(2,1)S(1)} %get-tuple-element.309), channel_id=1, source_target_pairs={{0,8},{1,9},{2,10},{3,11},{4,12},{5,13},{6,14},{7,15},{8,0},{9,1},... | collective-permute-start | bytes 221192 | tf_op jit(solution)/shard_map/cond/branch_1_fun/ppermute | solution.py:191
  193.8 1.4 collective-permute-start.10
  196.3 2.8 %branch_1_fun.14 = bf16[512,512]{1,0:T(8,128)(2,1)S(1)} custom-call(f32[512,128]{1,0:T(8,128)S(1)} %get-tuple-element.312.side_ref, f32[512,512]{1,0:T(8,128)} %get-tuple-element.313.hidden_ref, bf16[1536,512]{1,0:T(8,128)(2,1)} %bitcast.1.result_ref), custom_call_target="tpu_custom_call" | custom-call | flops 1 | bytes 1 | tf_op jit(solution)/shard_map/cond/branch_1_fun/pallas_call | solution.py:80
  199.1 3.0 %branch_1_fun.15 = (f32[512,512]{1,0:T(8,128)}, f32[512,512]{1,0:T(8,128)}) custom-call(f32[1024,512]{1,0:T(8,128)S(1)} %get-tuple-element.315.refs_0_, bf16[1024,512]{1,0:T(8,128)(2,1)S(1)} %collective-permute-done.12.refs_1_, bf16[1024,512]{1,0:T(8,128)(2,1)} %get-tuple-element.317.refs_2_), custom_call_target="tpu_custom_call" | custom-call | flops 1 | bytes 1 | tf_op jit(solution)/shard_map/cond/branch_1_fun/pallas_call | solution.py:80
  202.7 1.8 shard_map.226
  (65 shorter events, 13.3 us)
Async XLA Ops:
  2.2 9.8 %collective-permute-start.15 = (bf16[16,2304]{1,0:T(8,128)(2,1)S(1)}, bf16[16,2304]{1,0:T(8,128)(2,1)S(1)}, u32[]{:S(2)}, u32[]{:S(2)}) collective-permute-start(bf16[16,2304]{1,0:T(8,128)(2,1)S(1)} %get-tuple-element.210), channel_id=1, source_target_pairs={{0,24},{1,25},{2,26},{3,27},{4,28},{5,29},{6,30},{7,31},{8,16},{9,... | collective-permute-start | bytes 221192 | tf_op jit(solution)/shard_map/cond/branch_1_fun/ppermute | solution.py:191
  7.3 6.2 %collective-permute-start.14 = (bf16[16,2304]{1,0:T(8,128)(2,1)S(1)}, bf16[16,2304]{1,0:T(8,128)(2,1)S(1)}, u32[]{:S(2)}, u32[]{:S(2)}) collective-permute-start(bf16[16,2304]{1,0:T(8,128)(2,1)S(1)} %get-tuple-element.210), channel_id=1, source_target_pairs={{0,16},{1,17},{2,18},{3,19},{4,20},{5,21},{6,22},{7,23},{8,24},{9,... | collective-permute-start | bytes 221192 | tf_op jit(solution)/shard_map/cond/branch_1_fun/ppermute | solution.py:191
  7.3 6.2 %collective-permute-start.13 = (bf16[16,2304]{1,0:T(8,128)(2,1)S(1)}, bf16[16,2304]{1,0:T(8,128)(2,1)S(1)}, u32[]{:S(2)}, u32[]{:S(2)}) collective-permute-start(bf16[16,2304]{1,0:T(8,128)(2,1)S(1)} %get-tuple-element.210), channel_id=1, source_target_pairs={{0,8},{1,9},{2,10},{3,11},{4,12},{5,13},{6,14},{7,15},{8,0},{9,1},... | collective-permute-start | bytes 221192 | tf_op jit(solution)/shard_map/cond/branch_1_fun/ppermute | solution.py:191
  13.6 21.4 %copy-start.4 = (bf16[64,2304]{1,0:T(8,128)(2,1)}, bf16[64,2304]{1,0:T(8,128)(2,1)S(1)}, u32[]{:S(2)}) copy-start(bf16[64,2304]{1,0:T(8,128)(2,1)S(1)} %get-tuple-element.402.refs_0_) | copy-start | bytes 884740
  13.6 20.0 %copy-start = (bf16[1,512,512]{2,1,0:T(8,128)(2,1)S(1)}, bf16[1,512,512]{2,1,0:T(8,128)(2,1)}, u32[]{:S(2)}) copy-start(bf16[1,512,512]{2,1,0:T(8,128)(2,1)} %param.39) | copy-start | bytes 1572868
  13.6 40.7 %all-to-all-start.2 = ((bf16[4,2,192,512]{3,2,1,0:T(8,128)(2,1)}), bf16[4,2,192,512]{3,2,1,0:T(8,128)(2,1)S(1)}, u32[]{:S(2)}, u32[]{:S(2)}) async-start(bf16[4,2,192,512]{3,2,1,0:T(8,128)(2,1)} %get-tuple-element.408), calls=%async_computation.2 | async-start | bytes 3145728 | tf_op jit(solution)/shard_map/all_to_all | solution.py:916
  17.9 11.1 %collective-permute-start.28 = (bf16[64,2304]{1,0:T(8,128)(2,1)S(1)}, bf16[64,2304]{1,0:T(8,128)(2,1)}, u32[]{:S(2)}, u32[]{:S(2)}) collective-permute-start(bf16[64,2304]{1,0:T(8,128)(2,1)S(1)} %get-tuple-element.402.refs_0_), channel_id=1, source_target_pairs={{0,6},{1,7},{2,4},{3,5},{4,2},{5,3},{6,0},{7,1},{8,14},{9,15},{10,... | collective-permute-start | bytes 884744 | tf_op jit(solution)/shard_map/ppermute | solution.py:191
  20.4 13.1 %collective-permute-start.27 = (bf16[64,2304]{1,0:T(8,128)(2,1)S(1)}, bf16[64,2304]{1,0:T(8,128)(2,1)}, u32[]{:S(2)}, u32[]{:S(2)}) collective-permute-start(bf16[64,2304]{1,0:T(8,128)(2,1)S(1)} %get-tuple-element.402.refs_0_), channel_id=1, source_target_pairs={{0,4},{1,5},{2,6},{3,7},{4,0},{5,1},{6,2},{7,3},{8,12},{9,13},{10,... | collective-permute-start | bytes 884744 | tf_op jit(solution)/shard_map/ppermute | solution.py:191
  21.0 12.6 %collective-permute-start.26 = (bf16[64,2304]{1,0:T(8,128)(2,1)S(1)}, bf16[64,2304]{1,0:T(8,128)(2,1)}, u32[]{:S(2)}, u32[]{:S(2)}) collective-permute-start(bf16[64,2304]{1,0:T(8,128)(2,1)S(1)} %get-tuple-element.402.refs_0_), channel_id=1, source_target_pairs={{0,2},{1,3},{2,0},{3,1},{4,6},{5,7},{6,4},{7,5},{8,10},{9,11},{10,... | collective-permute-start | bytes 884744 | tf_op jit(solution)/shard_map/ppermute | solution.py:191
  33.6 18.7 %collective-permute-start.33 = (bf16[512,512]{1,0:T(8,128)(2,1)S(1)}, bf16[512,512]{1,0:T(8,128)(2,1)S(1)}, u32[]{:S(2)}, u32[]{:S(2)}) collective-permute-start(bf16[512,512]{1,0:T(8,128)(2,1)S(1)} %bitcast.19), channel_id=1, source_target_pairs={{0,2},{1,3},{2,0},{3,1},{4,6},{5,7},{6,4},{7,5},{8,10},{9,11},{10,... | collective-permute-start | bytes 1572872 | tf_op jit(solution)/shard_map/ppermute | solution.py:792
  35.0 2.1 %collective-permute-start.29 = (bf16[64,2304]{1,0:T(8,128)(2,1)S(1)}, bf16[64,2304]{1,0:T(8,128)(2,1)}, u32[]{:S(2)}, u32[]{:S(2)}) collective-permute-start(bf16[64,2304]{1,0:T(8,128)(2,1)S(1)} %get-tuple-element.402.refs_0_), channel_id=1, source_target_pairs={{0,1},{1,0},{2,3},{3,2},{4,5},{5,4},{6,7},{7,6},{8,9},{9,8},{10,11... | collective-permute-start | bytes 884744 | tf_op jit(solution)/shard_map/ppermute | solution.py:191
  35.0 2.3 %collective-permute-start.32 = (bf16[64,2304]{1,0:T(8,128)(2,1)}, bf16[64,2304]{1,0:T(8,128)(2,1)}, u32[]{:S(2)}, u32[]{:S(2)}) collective-permute-start(bf16[64,2304]{1,0:T(8,128)(2,1)} %collective-permute-done.28.refs_3_), channel_id=1, source_target_pairs={{0,1},{1,0},{2,3},{3,2},{4,5},{5,4},{6,7},{7,6},{8,9},{9,8},{10,11... | collective-permute-start | bytes 884744 | tf_op jit(solution)/shard_map/ppermute | solution.py:191
  35.5 2.3 %collective-permute-start.31 = (bf16[64,2304]{1,0:T(8,128)(2,1)}, bf16[64,2304]{1,0:T(8,128)(2,1)}, u32[]{:S(2)}, u32[]{:S(2)}) collective-permute-start(bf16[64,2304]{1,0:T(8,128)(2,1)} %collective-permute-done.27.refs_2_), channel_id=1, source_target_pairs={{0,1},{1,0},{2,3},{3,2},{4,5},{5,4},{6,7},{7,6},{8,9},{9,8},{10,11... | collective-permute-start | bytes 884744 | tf_op jit(solution)/shard_map/ppermute | solution.py:191
  35.5 2.7 %collective-permute-start.30 = (bf16[64,2304]{1,0:T(8,128)(2,1)}, bf16[64,2304]{1,0:T(8,128)(2,1)}, u32[]{:S(2)}, u32[]{:S(2)}) collective-permute-start(bf16[64,2304]{1,0:T(8,128)(2,1)} %collective-permute-done.26.refs_1_), channel_id=1, source_target_pairs={{0,1},{1,0},{2,3},{3,2},{4,5},{5,4},{6,7},{7,6},{8,9},{9,8},{10,11... | collective-permute-start | bytes 884744 | tf_op jit(solution)/shard_map/ppermute | solution.py:191
  38.2 16.1 %copy-start.1 = (bf16[1,512,512]{2,1,0:T(8,128)(2,1)S(1)}, bf16[1,512,512]{2,1,0:T(8,128)(2,1)}, u32[]{:S(2)}) copy-start(bf16[1,512,512]{2,1,0:T(8,128)(2,1)} %param.40) | copy-start | bytes 1572868
  54.3 25.4 %all-to-all-start.1 = ((bf16[4,208,512]{2,1,0:T(8,128)(2,1)}), bf16[4,208,512]{2,1,0:T(8,128)(2,1)}, u32[]{:S(2)}, u32[]{:S(2)}) async-start(bf16[4,208,512]{2,1,0:T(8,128)(2,1)} %get-tuple-element.218), calls=%async_computation.1 | async-start | bytes 1703936 | tf_op jit(solution)/shard_map/cond/branch_1_fun/all_to_all | solution.py:916
  58.5 13.1 %collective-permute-start.23 = (bf16[512,512]{1,0:T(8,128)(2,1)S(1)}, bf16[512,512]{1,0:T(8,128)(2,1)}, u32[]{:S(2)}, u32[]{:S(2)}) collective-permute-start(bf16[512,512]{1,0:T(8,128)(2,1)S(1)} %get-tuple-element.228.refs_6_), channel_id=1, source_target_pairs={{0,2},{1,3},{2,0},{3,1},{4,6},{5,7},{6,4},{7,5},{8,10},{9,11},{10,... | collective-permute-start | bytes 1572872 | tf_op jit(solution)/shard_map/cond/branch_1_fun/ppermute | solution.py:792
  61.3 36.8 %collective-permute-start.20 = (bf16[4,192,512]{2,1,0:T(8,128)(2,1)}, bf16[4,192,512]{2,1,0:T(8,128)(2,1)}, u32[]{:S(2)}, u32[]{:S(2)}) collective-permute-start(bf16[4,192,512]{2,1,0:T(8,128)(2,1)} %dynamic-slice_bitcast_fusion), channel_id=1, source_target_pairs={{0,4},{4,0},{8,12},{12,8},{16,20},{20,16},{24,28},{28,24},{1,5},{5... | collective-permute-start | bytes 2359304 | tf_op jit(solution)/shard_map/cond/branch_1_fun/ppermute | solution.py:797
  62.7 8.8 %collective-permute-start.21 = (bf16[512,512]{1,0:T(8,128)(2,1)S(1)}, bf16[512,512]{1,0:T(8,128)(2,1)}, u32[]{:S(2)}, u32[]{:S(2)}) collective-permute-start(bf16[512,512]{1,0:T(8,128)(2,1)S(1)} %get-tuple-element.226.refs_2_), channel_id=1, source_target_pairs={{0,1},{1,0},{2,3},{3,2},{4,5},{5,4},{6,7},{7,6},{8,9},{9,8},{10,11... | collective-permute-start | bytes 1572872 | tf_op jit(solution)/shard_map/cond/branch_1_fun/ppermute | solution.py:792
  62.8 10.5 %collective-permute-start.22 = (bf16[512,512]{1,0:T(8,128)(2,1)S(1)}, bf16[512,512]{1,0:T(8,128)(2,1)}, u32[]{:S(2)}, u32[]{:S(2)}) collective-permute-start(bf16[512,512]{1,0:T(8,128)(2,1)S(1)} %get-tuple-element.227.refs_4_), channel_id=1, source_target_pairs={{0,1},{1,0},{2,3},{3,2},{4,5},{5,4},{6,7},{7,6},{8,9},{9,8},{10,11... | collective-permute-start | bytes 1572872 | tf_op jit(solution)/shard_map/cond/branch_1_fun/ppermute | solution.py:792
  63.3 11.4 %collective-permute-start.24 = (bf16[512,512]{1,0:T(8,128)(2,1)S(1)}, bf16[512,512]{1,0:T(8,128)(2,1)}, u32[]{:S(2)}, u32[]{:S(2)}) collective-permute-start(bf16[512,512]{1,0:T(8,128)(2,1)S(1)} %get-tuple-element.228.refs_6_), channel_id=1, source_target_pairs={{0,1},{1,0},{2,3},{3,2},{4,5},{5,4},{6,7},{7,6},{8,9},{9,8},{10,11... | collective-permute-start | bytes 1572872 | tf_op jit(solution)/shard_map/cond/branch_1_fun/ppermute | solution.py:792
  71.6 6.6 %collective-permute-start.25 = (bf16[512,512]{1,0:T(8,128)(2,1)}, bf16[512,512]{1,0:T(8,128)(2,1)}, u32[]{:S(2)}, u32[]{:S(2)}) collective-permute-start(bf16[512,512]{1,0:T(8,128)(2,1)} %collective-permute-done.23.refs_8_), channel_id=1, source_target_pairs={{0,1},{1,0},{2,3},{3,2},{4,5},{5,4},{6,7},{7,6},{8,9},{9,8},{10,11... | collective-permute-start | bytes 1572872 | tf_op jit(solution)/shard_map/cond/branch_1_fun/ppermute | solution.py:792
  71.6 26.5 %collective-permute-start.16 = (bf16[208,512]{1,0:T(8,128)(2,1)}, bf16[208,512]{1,0:T(8,128)(2,1)}, u32[]{:S(2)}, u32[]{:S(2)}) collective-permute-start(bf16[208,512]{1,0:T(8,128)(2,1)} %get-tuple-element.219), channel_id=1, source_target_pairs={{0,4},{4,0},{8,12},{12,8},{16,20},{20,16},{24,28},{28,24},{1,5},{5... | collective-permute-start | bytes 638984 | tf_op jit(solution)/shard_map/cond/branch_1_fun/ppermute | solution.py:797
  73.3 24.8 %collective-permute-start.17 = (bf16[208,512]{1,0:T(8,128)(2,1)}, bf16[208,512]{1,0:T(8,128)(2,1)}, u32[]{:S(2)}, u32[]{:S(2)}) collective-permute-start(bf16[208,512]{1,0:T(8,128)(2,1)} %get-tuple-element.220), channel_id=1, source_target_pairs={{0,12},{4,8},{8,4},{12,0},{16,28},{20,24},{24,20},{28,16},{1,13},{... | collective-permute-start | bytes 638984 | tf_op jit(solution)/shard_map/cond/branch_1_fun/ppermute | solution.py:797
  74.7 23.4 %collective-permute-start.18 = (bf16[208,512]{1,0:T(8,128)(2,1)}, bf16[208,512]{1,0:T(8,128)(2,1)}, u32[]{:S(2)}, u32[]{:S(2)}) collective-permute-start(bf16[208,512]{1,0:T(8,128)(2,1)} %get-tuple-element.221), channel_id=1, source_target_pairs={{0,20},{4,16},{8,28},{12,24},{16,4},{20,0},{24,12},{28,8},{1,21},{... | collective-permute-start | bytes 638984 | tf_op jit(solution)/shard_map/cond/branch_1_fun/ppermute | solution.py:797
  78.2 19.9 %collective-permute-start.19 = (bf16[208,512]{1,0:T(8,128)(2,1)}, bf16[208,512]{1,0:T(8,128)(2,1)}, u32[]{:S(2)}, u32[]{:S(2)}) collective-permute-start(bf16[208,512]{1,0:T(8,128)(2,1)} %get-tuple-element.222), channel_id=1, source_target_pairs={{0,28},{4,24},{8,20},{12,16},{16,12},{20,8},{24,4},{28,0},{1,29},{... | collective-permute-start | bytes 638984 | tf_op jit(solution)/shard_map/cond/branch_1_fun/ppermute | solution.py:797
  98.3 40.2 %all-to-all-start = ((bf16[4,208,512]{2,1,0:T(8,128)(2,1)}), bf16[4,208,512]{2,1,0:T(8,128)(2,1)}, u32[]{:S(2)}, u32[]{:S(2)}) async-start(bf16[4,208,512]{2,1,0:T(8,128)(2,1)} %get-tuple-element.247), calls=%async_computation | async-start | bytes 1703936 | tf_op jit(solution)/shard_map/cond/branch_1_fun/all_to_all | solution.py:916
  114.7 23.3 %collective-permute-start.1 = (bf16[208,512]{1,0:T(8,128)(2,1)}, bf16[208,512]{1,0:T(8,128)(2,1)}, u32[]{:S(2)}, u32[]{:S(2)}) collective-permute-start(bf16[208,512]{1,0:T(8,128)(2,1)} %get-tuple-element.263), channel_id=1, source_target_pairs={{0,4},{4,0},{8,12},{12,8},{16,20},{20,16},{24,28},{28,24},{1,5},{5... | collective-permute-start | bytes 638984 | tf_op jit(solution)/shard_map/cond/branch_1_fun/ppermute | solution.py:797
  116.2 21.8 %collective-permute-start.2 = (bf16[208,512]{1,0:T(8,128)(2,1)}, bf16[208,512]{1,0:T(8,128)(2,1)}, u32[]{:S(2)}, u32[]{:S(2)}) collective-permute-start(bf16[208,512]{1,0:T(8,128)(2,1)} %get-tuple-element.264), channel_id=1, source_target_pairs={{0,12},{4,8},{8,4},{12,0},{16,28},{20,24},{24,20},{28,16},{1,13},{... | collective-permute-start | bytes 638984 | tf_op jit(solution)/shard_map/cond/branch_1_fun/ppermute | solution.py:797
  118.2 20.2 %collective-permute-start.3 = (bf16[208,512]{1,0:T(8,128)(2,1)}, bf16[208,512]{1,0:T(8,128)(2,1)}, u32[]{:S(2)}, u32[]{:S(2)}) collective-permute-start(bf16[208,512]{1,0:T(8,128)(2,1)} %get-tuple-element.265), channel_id=1, source_target_pairs={{0,20},{4,16},{8,28},{12,24},{16,4},{20,0},{24,12},{28,8},{1,21},{... | collective-permute-start | bytes 638984 | tf_op jit(solution)/shard_map/cond/branch_1_fun/ppermute | solution.py:797
  121.5 16.9 %collective-permute-start.4 = (bf16[208,512]{1,0:T(8,128)(2,1)}, bf16[208,512]{1,0:T(8,128)(2,1)}, u32[]{:S(2)}, u32[]{:S(2)}) collective-permute-start(bf16[208,512]{1,0:T(8,128)(2,1)} %get-tuple-element.266), channel_id=1, source_target_pairs={{0,28},{4,24},{8,20},{12,16},{16,12},{20,8},{24,4},{28,0},{1,29},{... | collective-permute-start | bytes 638984 | tf_op jit(solution)/shard_map/cond/branch_1_fun/ppermute | solution.py:797
  132.6 2.9 %collective-permute-start = (bf16[1024,512]{1,0:T(8,128)(2,1)}, bf16[1024,512]{1,0:T(8,128)(2,1)S(1)}, u32[]{:S(2)}, u32[]{:S(2)}) collective-permute-start(bf16[1024,512]{1,0:T(8,128)(2,1)} %get-tuple-element.246), channel_id=1, source_target_pairs={{0,1},{1,0},{2,3},{3,2},{4,5},{5,4},{6,7},{7,6},{8,9},{9,8},{10,11... | collective-permute-start | bytes 3145736 | tf_op jit(solution)/shard_map/cond/branch_1_fun/cond/branch_1_fun/ppermute | solution.py:792
  138.6 6.1 %copy-start.3 = (f32[512,512]{1,0:T(8,128)S(1)}, f32[512,512]{1,0:T(8,128)}, u32[]{:S(2)}) copy-start(f32[512,512]{1,0:T(8,128)} %get-tuple-element.432) | copy-start | bytes 3145732
  138.6 52.4 %all-to-all-start.3 = ((bf16[8,192,512]{2,1,0:T(8,128)(2,1)}), bf16[8,192,512]{2,1,0:T(8,128)(2,1)}, u32[]{:S(2)}, u32[]{:S(2)}) async-start(bf16[8,192,512]{2,1,0:T(8,128)(2,1)} %get-tuple-element.450), calls=%async_computation.3 | async-start | bytes 3145728 | tf_op jit(solution)/shard_map/all_to_all | solution.py:1009
  144.8 24.9 %collective-permute-start.5 = (bf16[1024,512]{1,0:T(8,128)(2,1)}, bf16[1024,512]{1,0:T(8,128)(2,1)}, u32[]{:S(2)}, u32[]{:S(2)}) collective-permute-start(bf16[1024,512]{1,0:T(8,128)(2,1)} %get-tuple-element.272), channel_id=1, source_target_pairs={{0,2},{1,3},{2,0},{3,1},{4,6},{5,7},{6,4},{7,5},{8,10},{9,11},{10,... | collective-permute-start | bytes 3145736 | tf_op jit(solution)/shard_map/cond/branch_1_fun/ppermute | solution.py:792
  169.6 2.8 %collective-permute-start.34 = (bf16[256,2304]{1,0:T(8,128)(2,1)S(1)}, bf16[256,2304]{1,0:T(8,128)(2,1)S(1)}, u32[]{:S(2)}, u32[]{:S(2)}) collective-permute-start(bf16[256,2304]{1,0:T(8,128)(2,1)S(1)} %get-tuple-element.437), channel_id=1, source_target_pairs={{0,1},{1,0},{2,3},{3,2},{4,5},{5,4},{6,7},{7,6},{8,9},{9,8},{10,11... | collective-permute-start | bytes 3538952 | tf_op jit(solution)/shard_map/ppermute | solution.py:191
  173.0 3.6 %copy-start.2 = (bf16[512,512]{1,0:T(8,128)(2,1)}, bf16[512,512]{1,0:T(8,128)(2,1)S(1)}, u32[]{:S(2)}) copy-start(bf16[512,512]{1,0:T(8,128)(2,1)S(1)} %get-tuple-element.305.refs_9_) | copy-start | bytes 1572868 | tf_op jit(solution)/shard_map/cond
  173.0 14.9 %collective-permute-start.6 = (bf16[64,2304]{1,0:T(8,128)(2,1)S(1)}, bf16[64,2304]{1,0:T(8,128)(2,1)}, u32[]{:S(2)}, u32[]{:S(2)}) collective-permute-start(bf16[64,2304]{1,0:T(8,128)(2,1)S(1)} %get-tuple-element.292), channel_id=1, source_target_pairs={{0,2},{1,3},{2,0},{3,1},{4,6},{5,7},{6,4},{7,5},{8,10},{9,11},{10,... | collective-permute-start | bytes 884744 | tf_op jit(solution)/shard_map/cond/branch_1_fun/ppermute | solution.py:191
  174.0 14.0 %collective-permute-start.7 = (bf16[64,2304]{1,0:T(8,128)(2,1)S(1)}, bf16[64,2304]{1,0:T(8,128)(2,1)}, u32[]{:S(2)}, u32[]{:S(2)}) collective-permute-start(bf16[64,2304]{1,0:T(8,128)(2,1)S(1)} %get-tuple-element.293), channel_id=1, source_target_pairs={{0,4},{1,5},{2,6},{3,7},{4,0},{5,1},{6,2},{7,3},{8,12},{9,13},{10,... | collective-permute-start | bytes 884744 | tf_op jit(solution)/shard_map/cond/branch_1_fun/ppermute | solution.py:191
  175.6 14.1 %collective-permute-start.8 = (bf16[64,2304]{1,0:T(8,128)(2,1)S(1)}, bf16[64,2304]{1,0:T(8,128)(2,1)}, u32[]{:S(2)}, u32[]{:S(2)}) collective-permute-start(bf16[64,2304]{1,0:T(8,128)(2,1)S(1)} %get-tuple-element.294), channel_id=1, source_target_pairs={{0,6},{1,7},{2,4},{3,5},{4,2},{5,3},{6,0},{7,1},{8,14},{9,15},{10,... | collective-permute-start | bytes 884744 | tf_op jit(solution)/shard_map/cond/branch_1_fun/ppermute | solution.py:191
  191.0 8.1 %collective-permute-start.12 = (bf16[1024,512]{1,0:T(8,128)(2,1)}, bf16[1024,512]{1,0:T(8,128)(2,1)S(1)}, u32[]{:S(2)}, u32[]{:S(2)}) collective-permute-start(bf16[1024,512]{1,0:T(8,128)(2,1)} %get-tuple-element.316), channel_id=1, source_target_pairs={{0,1},{1,0},{2,3},{3,2},{4,5},{5,4},{6,7},{7,6},{8,9},{9,8},{10,11... | collective-permute-start | bytes 3145736 | tf_op jit(solution)/shard_map/cond/branch_1_fun/ppermute | solution.py:792
  191.1 11.0 %collective-permute-start.9 = (bf16[16,2304]{1,0:T(8,128)(2,1)S(1)}, bf16[16,2304]{1,0:T(8,128)(2,1)}, u32[]{:S(2)}, u32[]{:S(2)}) collective-permute-start(bf16[16,2304]{1,0:T(8,128)(2,1)S(1)} %get-tuple-element.309), channel_id=1, source_target_pairs={{0,8},{1,9},{2,10},{3,11},{4,12},{5,13},{6,14},{7,15},{8,0},{9,1},... | collective-permute-start | bytes 221192 | tf_op jit(solution)/shard_map/cond/branch_1_fun/ppermute | solution.py:191
  193.8 8.8 %collective-permute-start.10 = (bf16[16,2304]{1,0:T(8,128)(2,1)S(1)}, bf16[16,2304]{1,0:T(8,128)(2,1)}, u32[]{:S(2)}, u32[]{:S(2)}) collective-permute-start(bf16[16,2304]{1,0:T(8,128)(2,1)S(1)} %get-tuple-element.310), channel_id=1, source_target_pairs={{0,16},{1,17},{2,18},{3,19},{4,20},{5,21},{6,22},{7,23},{8,24},{9,... | collective-permute-start | bytes 221192 | tf_op jit(solution)/shard_map/cond/branch_1_fun/ppermute | solution.py:191
  195.2 7.5 %collective-permute-start.11 = (bf16[16,2304]{1,0:T(8,128)(2,1)S(1)}, bf16[16,2304]{1,0:T(8,128)(2,1)}, u32[]{:S(2)}, u32[]{:S(2)}) collective-permute-start(bf16[16,2304]{1,0:T(8,128)(2,1)S(1)} %get-tuple-element.311), channel_id=1, source_target_pairs={{0,24},{1,25},{2,26},{3,27},{4,28},{5,29},{6,30},{7,31},{8,16},{9,... | collective-permute-start | bytes 221192 | tf_op jit(solution)/shard_map/cond/branch_1_fun/ppermute | solution.py:191
  202.7 1.8 copy-start.5
where the time goes:
time: 208 us; the launch traced here: 205 us
  Pallas kernels  94.5 us (45%)
  starting transfers between devices  59 us (28%)
  waiting for transfers between devices  44.9 us (22%)
  other arithmetic  2.5 us (1%)
    pallas_call x13, Pallas kernels, call(): pl.pallas_call(kernel, out_shape=outs, in_specs=[spec(at) for at in range...  94.5 us
    ppermute x17, waiting for transfers between devices, swap(): lax.ppermute(value, BOTH, [(i, i ^ mask) for i in range(self.devices)])  20.9 us
    ppermute x17, starting transfers between devices, swap(): lax.ppermute(value, BOTH, [(i, i ^ mask) for i in range(self.devices)])  19 us
    ppermute x9, starting transfers between devices, swap_expert(): return lax.ppermute(value, 'expert', [(i, i ^ mask) for i in range(size)])  15.2 us
    all_to_all x3, starting transfers between devices, exchange_even(): lax.all_to_all(value, 'expert', split_axis=0, concat_axis=0, axis_index_g...  13.2 us
    ppermute x9, waiting for transfers between devices, swap_hidden(): return lax.ppermute(value, 'hidden', [(i, i ^ mask) for i in range(size)])  13.2 us
    ppermute x9, waiting for transfers between devices, swap_expert(): return lax.ppermute(value, 'expert', [(i, i ^ mask) for i in range(size)])  7.42 us
    all_to_all x1, starting transfers between devices, body(): lax.all_to_all(after(result, back), 'expert', split_axis=0, concat_axis=0...  6.13 us
  transfers between devices with their start and end apart: 39, of which 17 were waited for; matrix products, arithmetic and copies ran while one was open for 2% of the time, Pallas kernels for 45%

commit v1 on v0

--- a/solution.py
+++ b/solution.py
@@ -1015,7 +1015,7 @@
         dense_shapes = [shape((width, wide), F32)]
     cfg.dense_outs = len(dense_shapes)
 
-    def back_part(value, back):
+    def back_kernel_part(back):
         args = [me, side, rows, gates, lse] + back + [hidden_one, cotangent, heads, tokens, proj, full]
         outs = call(
             functools.partial(backward_kernel, cfg),
@@ -1048,7 +1048,10 @@
             far_in=range(5, len(args)),
             far_out=range(1 + len(dense_shapes)),
         )
-        return swap_hidden(value, hidden // 2), outs
+        return (*outs[:2], groups.swap(outs[2], 1)) if staged else tuple(outs)
+
+    def back_part(value, back):
+        return swap_hidden(value, hidden // 2), apart(always, back_kernel_part, back)
 
     last, outs = apart(always, back_part, value, back)
     reached = held + [last]
@@ -1080,7 +1083,7 @@
 
     blocks = [None]
     if staged:
-        blocks = add_parts(outs[1], [groups.swap(outs[2], 1)], len(groups.mid))
+        blocks = add_parts(outs[1], [outs[2]], len(groups.mid))
     got, (own, more) = apart(always, last_weights, blocks)
     if staged:
         blocks = add_parts(blocks[0], got, len(groups.far))

time: 208 us -> 215 us (1.034); the launches traced: 205 us -> 218 us
  starting transfers between devices: 59 us -> 72.9 us
    all_to_all x3, starting transfers between devices: 13.2 us -> 26.5 us  [exchange_even(): lax.all_to_all(value, 'expert', split_axis=0, concat_axis=0, axis_index_g...]
  transfers between devices with their start and end apart: 39 -> 39, of which waited for: 17 -> 17; matrix products, arithmetic and copies ran while one was open for 2% -> 2% of each run, Pallas kernels for 45% -> 42%
where the time goes in v1:
time: 215 us; the launch traced here: 218 us
  Pallas kernels  94.9 us (44%)
  starting transfers between devices  72.9 us (34%)
  waiting for transfers between devices  43.5 us (20%)
  other arithmetic  2.51 us (1%)
    pallas_call x13, Pallas kernels, call(): pl.pallas_call(kernel, out_shape=outs, in_specs=[spec(at) for at in range...  94.9 us
    all_to_all x3, starting transfers between devices, exchange_even(): lax.all_to_all(value, 'expert', split_axis=0, concat_axis=0, axis_index_g...  26.5 us
    ppermute x17, waiting for transfers between devices, swap(): lax.ppermute(value, BOTH, [(i, i ^ mask) for i in range(self.devices)])  21.7 us
    ppermute x17, starting transfers between devices, swap(): lax.ppermute(value, BOTH, [(i, i ^ mask) for i in range(self.devices)])  19.7 us
    ppermute x9, starting transfers between devices, swap_expert(): return lax.ppermute(value, 'expert', [(i, i ^ mask) for i in range(size)])  15.1 us
    ppermute x9, waiting for transfers between devices, swap_hidden(): return lax.ppermute(value, 'hidden', [(i, i ^ mask) for i in range(size)])  13 us
    ppermute x9, waiting for transfers between devices, swap_expert(): return lax.ppermute(value, 'expert', [(i, i ^ mask) for i in range(size)])  6.64 us
    all_to_all x1, starting transfers between devices, body(): lax.all_to_all(after(result, back), 'expert', split_axis=0, concat_axis=0...  6.47 us
  transfers between devices with their start and end apart: 39, of which 17 were waited for; matrix products, arithmetic and copies ran while one was open for 2% of the time, Pallas kernels for 42%

profile of v1, /device:TPU:0, one launch (start us, length us, event | category | flops | bytes accessed | tf_op | source)
XLA Modules:
  0.0 217.7 jit_solution(5088086782077654047)
XLA Ops:
  2.2 11.3 %conditional.8 = (bf16[64,2304]{1,0:T(8,128)(2,1)S(1)}, f32[512,128]{1,0:T(8,128)S(1)}, f32[8,512]{1,0:T(8,128)S(1)}, bf16[4,2,192,512]{3,2,1,0:T(8,128)(2,1)}) conditional(s32[]{:T(128)} %convert_element_type.8, () %tuple.83, (bf16[16,2304]{1,0:T(8,128)(2,1)S(1)}, s32[1,16]{1,0:T(1,128)}, s32[1,16]{1,0:T(1,128)}, s32[2,512]{1,0:T(2,128)}, ...), branch_computations={%region_0.0_spmd, %region_1.0_spmd} | conditional | flops 1179649 | bytes 2146348 | solution.py:787
  2.2 5.1 %collective-permute-start.16 = (bf16[16,2304]{1,0:T(8,128)(2,1)S(1)}, bf16[16,2304]{1,0:T(8,128)(2,1)S(1)}, u32[]{:S(2)}, u32[]{:S(2)}) collective-permute-start(bf16[16,2304]{1,0:T(8,128)(2,1)S(1)} %get-tuple-element.244), channel_id=1, source_target_pairs={{0,24},{1,25},{2,26},{3,27},{4,28},{5,29},{6,30},{7,31},{8,16},{9,... | collective-permute-start | bytes 221192 | tf_op jit(solution)/shard_map/cond/branch_1_fun/ppermute | solution.py:191
  8.0 4.1 %branch_1_fun.8 = (f32[512,128]{1,0:T(8,128)S(1)}, f32[8,512]{1,0:T(8,128)S(1)}, bf16[4,2,192,512]{3,2,1,0:T(8,128)(2,1)}) custom-call(s32[1,16]{1,0:T(1,128)} %get-tuple-element.245.lens_ref, s32[1,16]{1,0:T(1,128)} %get-tuple-element.524.tasks_ref, s32[2,512]{1,0:T(2,128)} %get-tuple-element.247.routes_ref, bf16[512,512]{1,0:T(8,128)(2,1)} %get-tuple-element.248.cot_in), custom_call_target="tpu_custom_call" | custom-call | flops 1 | bytes 1 | tf_op jit(solution)/shard_map/cond/branch_1_fun/pallas_call | solution.py:80
  12.1 1.5 collective-permute-done.15
  13.6 17.6 %all-to-all-start.2 = ((bf16[4,2,192,512]{3,2,1,0:T(8,128)(2,1)}), bf16[4,2,192,512]{3,2,1,0:T(8,128)(2,1)S(1)}, u32[]{:S(2)}, u32[]{:S(2)}) async-start(bf16[4,2,192,512]{3,2,1,0:T(8,128)(2,1)} %get-tuple-element.462), calls=%async_computation.2 | async-start | bytes 3145728 | tf_op jit(solution)/shard_map/all_to_all | solution.py:916
  31.2 2.5 %collective-permute-start.29 = (bf16[64,2304]{1,0:T(8,128)(2,1)S(1)}, bf16[64,2304]{1,0:T(8,128)(2,1)}, u32[]{:S(2)}, u32[]{:S(2)}) collective-permute-start(bf16[64,2304]{1,0:T(8,128)(2,1)S(1)} %get-tuple-element.456.refs_0_), channel_id=1, source_target_pairs={{0,6},{1,7},{2,4},{3,5},{4,2},{5,3},{6,0},{7,1},{8,14},{9,15},{10,... | collective-permute-start | bytes 884744 | tf_op jit(solution)/shard_map/ppermute | solution.py:191
  34.8 7.5 %collective-permute-done.29.refs_3_ = bf16[64,2304]{1,0:T(8,128)(2,1)} collective-permute-done((bf16[64,2304]{1,0:T(8,128)(2,1)S(1)}, bf16[64,2304]{1,0:T(8,128)(2,1)}, u32[]{:S(2)}, u32[]{:S(2)}) %collective-permute-start.29) | collective-permute-done | bytes 294944 | tf_op jit(solution)/shard_map/ppermute | solution.py:191
  42.3 4.9 %collective-permute-done.28.refs_2_ = bf16[64,2304]{1,0:T(8,128)(2,1)} collective-permute-done((bf16[64,2304]{1,0:T(8,128)(2,1)S(1)}, bf16[64,2304]{1,0:T(8,128)(2,1)}, u32[]{:S(2)}, u32[]{:S(2)}) %collective-permute-start.28) | collective-permute-done | bytes 294944 | tf_op jit(solution)/shard_map/ppermute | solution.py:191
  47.2 1.4 collective-permute-start.34
  51.8 15.2 %shard_map.223 = (bf16[512,2304]{1,0:T(8,128)(2,1)}, bf16[512,1536]{1,0:T(8,128)(2,1)}, bf16[512,512]{1,0:T(8,128)(2,1)}, f32[8,512]{1,0:T(8,128)S(1)}, f32[512,...) custom-call(s32[1]{0:T(128)} %bitcast.5.me_ref, ...), custom_call_target="tpu_custom_call" | custom-call | flops 1 | bytes 1 | tf_op jit(solution)/shard_map/pallas_call | solution.py:80
  67.6 44.0 %conditional.9 = (bf16[4,208,512]{2,1,0:T(8,128)(2,1)}, bf16[208,512]{1,0:T(8,128)(2,1)}, bf16[208,512]{1,0:T(8,128)(2,1)}, bf16[208,512]{1,0:T(8,128)(2,1)}, bf...) conditional(s32[]{:T(128)} %convert_element_type.8, () %tuple.82, ...), branch_computations={%region_2.3_spmd, %region_3.4_spmd} | conditional | flops 16 | bytes 21168832 | solution.py:787
  67.6 4.2 %all-to-all-start.1 = ((bf16[4,208,512]{2,1,0:T(8,128)(2,1)}), bf16[4,208,512]{2,1,0:T(8,128)(2,1)}, u32[]{:S(2)}, u32[]{:S(2)}) async-start(bf16[4,208,512]{2,1,0:T(8,128)(2,1)} %get-tuple-element.252), calls=%async_computation.1 | async-start | bytes 1703936 | tf_op jit(solution)/shard_map/cond/branch_1_fun/all_to_all | solution.py:916
  71.8 1.8 collective-permute-start.24
  74.6 1.5 collective-permute-start.21
  76.6 8.8 %collective-permute-done.24.refs_8_ = bf16[512,512]{1,0:T(8,128)(2,1)} collective-permute-done((bf16[512,512]{1,0:T(8,128)(2,1)S(1)}, bf16[512,512]{1,0:T(8,128)(2,1)}, u32[]{:S(2)}, u32[]{:S(2)}) %collective-permute-start.24) | collective-permute-done | bytes 524320 | tf_op jit(solution)/shard_map/cond/branch_1_fun/ppermute | solution.py:792
  85.4 1.5 collective-permute-start.17
  86.9 1.6 collective-permute-start.18
  88.5 3.3 %collective-permute-start.19 = (bf16[208,512]{1,0:T(8,128)(2,1)}, bf16[208,512]{1,0:T(8,128)(2,1)}, u32[]{:S(2)}, u32[]{:S(2)}) collective-permute-start(bf16[208,512]{1,0:T(8,128)(2,1)} %get-tuple-element.255), channel_id=1, source_target_pairs={{0,20},{4,16},{8,28},{12,24},{16,4},{20,0},{24,12},{28,8},{1,21},{... | collective-permute-start | bytes 638984 | tf_op jit(solution)/shard_map/cond/branch_1_fun/ppermute | solution.py:797
  92.2 1.6 all-to-all-done.1.refs_1_
  93.7 11.4 %branch_1_fun.9 = (bf16[4,192,512]{2,1,0:T(8,128)(2,1)}, bf16[4,208,512]{2,1,0:T(8,128)(2,1)}, bf16[768,512]{1,0:T(8,128)(2,1)}) custom-call(s32[1]{0:T(128)} %get-tuple-element.263.me_ref, bf16[4,2,192,512]{3,2,1,0:T(8,128)(2,1)S(1)} %get-tuple-element.257.refs_0_, bf16[4,208,512]{2,1,0:T(8,128)(2,1)} %all-to-all-done.1.refs_1_, ...), custom_call_target="tpu_custom_call" | custom-call | flops 1 | bytes 1 | tf_op jit(solution)/shard_map/cond/branch_1_fun/pallas_call | solution.py:80
  105.2 6.2 %collective-permute-done.17 = bf16[208,512]{1,0:T(8,128)(2,1)} collective-permute-done((bf16[208,512]{1,0:T(8,128)(2,1)}, bf16[208,512]{1,0:T(8,128)(2,1)}, u32[]{:S(2)}, u32[]{:S(2)}) %collective-permute-start.17) | collective-permute-done | bytes 213024 | tf_op jit(solution)/shard_map/cond/branch_1_fun/ppermute | solution.py:797
  111.6 40.3 %conditional.10 = (bf16[4,208,512]{2,1,0:T(8,128)(2,1)}, bf16[208,512]{1,0:T(8,128)(2,1)}, bf16[208,512]{1,0:T(8,128)(2,1)}, bf16[208,512]{1,0:T(8,128)(2,1)}, b...) conditional(s32[]{:T(128)} %convert_element_type.8, () %tuple.81, ...), branch_computations={%region_4.5_spmd, %region_5.8_spmd} | conditional | flops 524291 | bytes 13304215 | solution.py:787
  111.6 4.7 %all-to-all-start = ((bf16[4,208,512]{2,1,0:T(8,128)(2,1)}), bf16[4,208,512]{2,1,0:T(8,128)(2,1)}, u32[]{:S(2)}, u32[]{:S(2)}) async-start(bf16[4,208,512]{2,1,0:T(8,128)(2,1)} %get-tuple-element.281), calls=%async_computation | async-start | bytes 1703936 | tf_op jit(solution)/shard_map/cond/branch_1_fun/all_to_all | solution.py:916
  116.3 11.6 %branch_1_fun.11 = (bf16[8,192,512]{2,1,0:T(8,128)(2,1)}, bf16[208,512]{1,0:T(8,128)(2,1)}, bf16[208,512]{1,0:T(8,128)(2,1)}, bf16[208,512]{1,0:T(8,128)(2,1)}, ...) custom-call(s32[1]{0:T(128)} %get-tuple-element.282.me_ref, bf16[4,192,512]{2,1,0:T(8,128)(2,1)} %get-tuple-element.283.refs_0_, ...), custom_call_target="tpu_custom_call" | custom-call | flops 1 | bytes 1 | tf_op jit(solution)/shard_map/cond/branch_1_fun/pallas_call | solution.py:80
  128.0 1.5 collective-permute-start.1
  129.5 2.0 collective-permute-start.2
  131.5 3.3 %collective-permute-start.3 = (bf16[208,512]{1,0:T(8,128)(2,1)}, bf16[208,512]{1,0:T(8,128)(2,1)}, u32[]{:S(2)}, u32[]{:S(2)}) collective-permute-start(bf16[208,512]{1,0:T(8,128)(2,1)} %get-tuple-element.299), channel_id=1, source_target_pairs={{0,20},{4,16},{8,28},{12,24},{16,4},{20,0},{24,12},{28,8},{1,21},{... | collective-permute-start | bytes 638984 | tf_op jit(solution)/shard_map/cond/branch_1_fun/ppermute | solution.py:797
  134.9 16.4 %conditional = (bf16[1024,512]{1,0:T(8,128)(2,1)}) conditional(s32[]{:T(128)} %convert_element_type.1, () %tuple.50, (s32[1]{0:T(128)}, bf16[4,208,512]{2,1,0:T(8,128)(2,1)}, bf16[208,512]{1,0:T(8,128)(2,1)}, bf16[208,512]{1,0:T(8,128)(2,1)}, bf16[208,512]{1,0:T(8,128)(2,1)}, /*index=5*/bf16[208,512]{1,0:T(8,128)(2,1)}, bf16[768,512]{1,0:T(8,128)(2,1)}, ...), branch_computations={%region_6.6_spmd, %region_7.7_spmd} | conditional | flops 524289 | bytes 7340081 | solution.py:787
  135.2 10.6 %branch_1_fun.10 = (bf16[1024,512]{1,0:T(8,128)(2,1)}, bf16[1024,512]{1,0:T(8,128)(2,1)}) custom-call(s32[1]{0:T(128)} %get-tuple-element.267.me_ref, bf16[4,208,512]{2,1,0:T(8,128)(2,1)} %get-tuple-element.268.refs_0_, bf16[208,512]{1,0:T(8,128)(2,1)} %get-tuple-element.269.refs_1_, bf16[208,512]{1,0:T(8,128)(2,1)} %get-tuple-element.270.refs_2_, ...), custom_call_target="tpu_custom_call" | custom-call | flops 1 | bytes 1 | tf_op jit(solution)/shard_map/cond/branch_1_fun/cond/branch_1_fun/pallas_call | solution.py:80
  145.9 2.9 %collective-permute-done = bf16[1024,512]{1,0:T(8,128)(2,1)S(1)} collective-permute-done((bf16[1024,512]{1,0:T(8,128)(2,1)}, bf16[1024,512]{1,0:T(8,128)(2,1)S(1)}, u32[]{:S(2)}, u32[]{:S(2)}) %collective-permute-start) | collective-permute-done | bytes 1048608 | tf_op jit(solution)/shard_map/cond/branch_1_fun/cond/branch_1_fun/ppermute | solution.py:792
  148.8 2.5 %add.14 = bf16[1024,512]{1,0:T(8,128)(2,1)} add(bf16[1024,512]{1,0:T(8,128)(2,1)} %get-tuple-element.279, bf16[1024,512]{1,0:T(8,128)(2,1)S(1)} %collective-permute-done) | non-fusion elementwise | flops 524288 | bytes 3145728 | tf_op jit(solution)/shard_map/cond/branch_1_fun/cond/branch_1_fun/add | solution.py:825
  152.0 6.5 %all-to-all-start.3 = ((bf16[8,192,512]{2,1,0:T(8,128)(2,1)}), bf16[8,192,512]{2,1,0:T(8,128)(2,1)}, u32[]{:S(2)}, u32[]{:S(2)}) async-start(bf16[8,192,512]{2,1,0:T(8,128)(2,1)} %get-tuple-element.504), calls=%async_computation.3 | async-start | bytes 3145728 | tf_op jit(solution)/shard_map/all_to_all | solution.py:1009
  158.5 24.6 %conditional.11 = (bf16[1024,512]{1,0:T(8,128)(2,1)}, f32[512,512]{1,0:T(8,128)}, bf16[256,2304]{1,0:T(8,128)(2,1)}, bf16[256,2304]{1,0:T(8,128)(2,1)}) conditional(s32[]{:T(128)} %convert_element_type.8, () %tuple.80, (bf16[1024,512]{1,0:T(8,128)(2,1)}, pred[]{:T(512)}, s32[1]{0:T(128)}, f32[512,128]{1,0:T(8,128)S(1)}, f32[8,512]{1,0:T(8,128)S(1)}, ...), branch_computations={%region_8.9_spmd, %region_9.12_spmd} | conditional | flops 2 | bytes 8913166 | solution.py:787
  159.7 22.1 %conditional.1 = (f32[512,512]{1,0:T(8,128)}, bf16[256,2304]{1,0:T(8,128)(2,1)}, bf16[256,2304]{1,0:T(8,128)(2,1)}) conditional(s32[]{:T(128)} %convert_element_type.3, () %tuple.56, (s32[1]{0:T(128)}, f32[512,128]{1,0:T(8,128)S(1)}, f32[8,512]{1,0:T(8,128)S(1)}, f32[512,128]{1,0:T(8,128)}, f32[8,512]{1,0:T(8,128)S(1)}, ...), branch_computations={%region_10.10_spmd, %region_11.11_spmd} | conditional | flops 1 | bytes 4718657 | solution.py:787
  159.7 18.8 %branch_1_fun.12 = (f32[512,512]{1,0:T(8,128)}, bf16[256,2304]{1,0:T(8,128)(2,1)}, bf16[256,2304]{1,0:T(8,128)(2,1)}) custom-call(s32[1]{0:T(128)} %get-tuple-element.306.me_ref, f32[512,128]{1,0:T(8,128)S(1)} %get-tuple-element.307.side_ref, f32[8,512]{1,0:T(8,128)S(1)} %get-tuple-element.308.rows_ref, f32[512,128]{1,0:T(8,128)} %get-tuple-element.309.gates_ref, ...), custom_call_target="tpu_custom_call" | custom-call | flops 1 | bytes 1 | tf_op jit(solution)/shard_map/cond/branch_1_fun/cond/branch_1_fun/pallas_call | solution.py:80
  178.6 3.2 %collective-permute-done.5 = bf16[256,2304]{1,0:T(8,128)(2,1)} collective-permute-done((bf16[256,2304]{1,0:T(8,128)(2,1)}, bf16[256,2304]{1,0:T(8,128)(2,1)}, u32[]{:S(2)}, u32[]{:S(2)}) %collective-permute-start.5) | collective-permute-done | bytes 1179680 | tf_op jit(solution)/shard_map/cond/branch_1_fun/cond/branch_1_fun/ppermute | solution.py:191
  181.8 1.3 collective-permute-done.6
  183.0 1.9 shard_map.224
  184.9 17.2 %conditional.12 = (bf16[64,2304]{1,0:T(8,128)(2,1)}, bf16[64,2304]{1,0:T(8,128)(2,1)}, bf16[64,2304]{1,0:T(8,128)(2,1)}, f32[1024,512]{1,0:T(8,128)S(1)}, bf16[1024,512]{1,0:T(8,128)(2,1)}) conditional(s32[]{:T(128)} %convert_element_type.8, () %tuple.89, (bf16[64,2304]{1,0:T(8,128)(2,1)S(1)}, bf16[64,2304]{1,0:T(8,128)(2,1)S(1)}, ...), branch_computations={%region_12.13_spmd, %region_13.14_spmd} | conditional | flops 1 | bytes 5636285 | solution.py:787
  186.2 1.7 collective-permute-start.8
  188.7 11.4 %branch_1_fun.13 = (f32[1024,512]{1,0:T(8,128)S(1)}, bf16[1024,512]{1,0:T(8,128)(2,1)}) custom-call(s32[1]{0:T(128)} %get-tuple-element.349.me_ref, bf16[4,208,512]{2,1,0:T(8,128)(2,1)} %get-tuple-element.350.refs_0_, bf16[208,512]{1,0:T(8,128)(2,1)} %get-tuple-element.351.refs_1_, bf16[208,512]{1,0:T(8,128)(2,1)} %get-tuple-element.352.refs_2_, ...), custom_call_target="tpu_custom_call" | custom-call | flops 1 | bytes 1 | tf_op jit(solution)/shard_map/cond/branch_1_fun/pallas_call | solution.py:80
  200.2 1.9 collective-permute-done.9
  203.4 12.2 %conditional.13 = (bf16[16,2304]{1,0:T(8,128)(2,1)}, bf16[16,2304]{1,0:T(8,128)(2,1)}, bf16[16,2304]{1,0:T(8,128)(2,1)}, bf16[512,512]{1,0:T(8,128)(2,1)S(1)}, f...) conditional(s32[]{:T(128)} %convert_element_type.8, () %tuple.79, (bf16[16,2304]{1,0:T(8,128)(2,1)S(1)}, ...), branch_computations={%region_14.15_spmd, %region_15.16_spmd} | conditional | flops 2 | bytes 5079250 | solution.py:787
  203.5 3.3 %collective-permute-start.10 = (bf16[16,2304]{1,0:T(8,128)(2,1)S(1)}, bf16[16,2304]{1,0:T(8,128)(2,1)}, u32[]{:S(2)}, u32[]{:S(2)}) collective-permute-start(bf16[16,2304]{1,0:T(8,128)(2,1)S(1)} %get-tuple-element.363), channel_id=1, source_target_pairs={{0,8},{1,9},{2,10},{3,11},{4,12},{5,13},{6,14},{7,15},{8,0},{9,1},... | collective-permute-start | bytes 221192 | tf_op jit(solution)/shard_map/cond/branch_1_fun/ppermute | solution.py:191
  206.8 2.4 %collective-permute-start.12 = (bf16[16,2304]{1,0:T(8,128)(2,1)S(1)}, bf16[16,2304]{1,0:T(8,128)(2,1)}, u32[]{:S(2)}, u32[]{:S(2)}) collective-permute-start(bf16[16,2304]{1,0:T(8,128)(2,1)S(1)} %get-tuple-element.365), channel_id=1, source_target_pairs={{0,24},{1,25},{2,26},{3,27},{4,28},{5,29},{6,30},{7,31},{8,16},{9,... | collective-permute-start | bytes 221192 | tf_op jit(solution)/shard_map/cond/branch_1_fun/ppermute | solution.py:191
  209.2 2.8 %branch_1_fun.14 = bf16[512,512]{1,0:T(8,128)(2,1)S(1)} custom-call(f32[512,128]{1,0:T(8,128)S(1)} %get-tuple-element.366.side_ref, f32[512,512]{1,0:T(8,128)} %get-tuple-element.367.hidden_ref, bf16[1536,512]{1,0:T(8,128)(2,1)} %bitcast.1.result_ref), custom_call_target="tpu_custom_call" | custom-call | flops 1 | bytes 1 | tf_op jit(solution)/shard_map/cond/branch_1_fun/pallas_call | solution.py:80
  212.0 3.0 %branch_1_fun.15 = (f32[512,512]{1,0:T(8,128)}, f32[512,512]{1,0:T(8,128)}) custom-call(f32[1024,512]{1,0:T(8,128)S(1)} %get-tuple-element.369.refs_0_, bf16[1024,512]{1,0:T(8,128)(2,1)S(1)} %collective-permute-done.13.refs_1_, bf16[1024,512]{1,0:T(8,128)(2,1)} %get-tuple-element.371.refs_2_), custom_call_target="tpu_custom_call" | custom-call | flops 1 | bytes 1 | tf_op jit(solution)/shard_map/cond/branch_1_fun/pallas_call | solution.py:80
  215.6 1.8 shard_map.226
  (70 shorter events, 14.0 us)
Async XLA Ops:
  2.2 9.8 %collective-permute-start.16 = (bf16[16,2304]{1,0:T(8,128)(2,1)S(1)}, bf16[16,2304]{1,0:T(8,128)(2,1)S(1)}, u32[]{:S(2)}, u32[]{:S(2)}) collective-permute-start(bf16[16,2304]{1,0:T(8,128)(2,1)S(1)} %get-tuple-element.244), channel_id=1, source_target_pairs={{0,24},{1,25},{2,26},{3,27},{4,28},{5,29},{6,30},{7,31},{8,16},{9,... | collective-permute-start | bytes 221192 | tf_op jit(solution)/shard_map/cond/branch_1_fun/ppermute | solution.py:191
  7.3 6.2 %collective-permute-start.15 = (bf16[16,2304]{1,0:T(8,128)(2,1)S(1)}, bf16[16,2304]{1,0:T(8,128)(2,1)S(1)}, u32[]{:S(2)}, u32[]{:S(2)}) collective-permute-start(bf16[16,2304]{1,0:T(8,128)(2,1)S(1)} %get-tuple-element.244), channel_id=1, source_target_pairs={{0,16},{1,17},{2,18},{3,19},{4,20},{5,21},{6,22},{7,23},{8,24},{9,... | collective-permute-start | bytes 221192 | tf_op jit(solution)/shard_map/cond/branch_1_fun/ppermute | solution.py:191
  7.3 6.2 %collective-permute-start.14 = (bf16[16,2304]{1,0:T(8,128)(2,1)S(1)}, bf16[16,2304]{1,0:T(8,128)(2,1)S(1)}, u32[]{:S(2)}, u32[]{:S(2)}) collective-permute-start(bf16[16,2304]{1,0:T(8,128)(2,1)S(1)} %get-tuple-element.244), channel_id=1, source_target_pairs={{0,8},{1,9},{2,10},{3,11},{4,12},{5,13},{6,14},{7,15},{8,0},{9,1},... | collective-permute-start | bytes 221192 | tf_op jit(solution)/shard_map/cond/branch_1_fun/ppermute | solution.py:191
  13.6 35.0 %copy-start.6 = (bf16[64,2304]{1,0:T(8,128)(2,1)}, bf16[64,2304]{1,0:T(8,128)(2,1)S(1)}, u32[]{:S(2)}) copy-start(bf16[64,2304]{1,0:T(8,128)(2,1)S(1)} %get-tuple-element.456.refs_0_) | copy-start | bytes 884740
  13.6 33.6 %copy-start = (bf16[1,512,512]{2,1,0:T(8,128)(2,1)S(1)}, bf16[1,512,512]{2,1,0:T(8,128)(2,1)}, u32[]{:S(2)}) copy-start(bf16[1,512,512]{2,1,0:T(8,128)(2,1)} %param.41) | copy-start | bytes 1572868
  13.6 54.0 %all-to-all-start.2 = ((bf16[4,2,192,512]{3,2,1,0:T(8,128)(2,1)}), bf16[4,2,192,512]{3,2,1,0:T(8,128)(2,1)S(1)}, u32[]{:S(2)}, u32[]{:S(2)}) async-start(bf16[4,2,192,512]{3,2,1,0:T(8,128)(2,1)} %get-tuple-element.462), calls=%async_computation.2 | async-start | bytes 3145728 | tf_op jit(solution)/shard_map/all_to_all | solution.py:916
  31.2 11.1 %collective-permute-start.29 = (bf16[64,2304]{1,0:T(8,128)(2,1)S(1)}, bf16[64,2304]{1,0:T(8,128)(2,1)}, u32[]{:S(2)}, u32[]{:S(2)}) collective-permute-start(bf16[64,2304]{1,0:T(8,128)(2,1)S(1)} %get-tuple-element.456.refs_0_), channel_id=1, source_target_pairs={{0,6},{1,7},{2,4},{3,5},{4,2},{5,3},{6,0},{7,1},{8,14},{9,15},{10,... | collective-permute-start | bytes 884744 | tf_op jit(solution)/shard_map/ppermute | solution.py:191
  33.8 13.4 %collective-permute-start.28 = (bf16[64,2304]{1,0:T(8,128)(2,1)S(1)}, bf16[64,2304]{1,0:T(8,128)(2,1)}, u32[]{:S(2)}, u32[]{:S(2)}) collective-permute-start(bf16[64,2304]{1,0:T(8,128)(2,1)S(1)} %get-tuple-element.456.refs_0_), channel_id=1, source_target_pairs={{0,4},{1,5},{2,6},{3,7},{4,0},{5,1},{6,2},{7,3},{8,12},{9,13},{10,... | collective-permute-start | bytes 884744 | tf_op jit(solution)/shard_map/ppermute | solution.py:191
  34.3 12.9 %collective-permute-start.27 = (bf16[64,2304]{1,0:T(8,128)(2,1)S(1)}, bf16[64,2304]{1,0:T(8,128)(2,1)}, u32[]{:S(2)}, u32[]{:S(2)}) collective-permute-start(bf16[64,2304]{1,0:T(8,128)(2,1)S(1)} %get-tuple-element.456.refs_0_), channel_id=1, source_target_pairs={{0,2},{1,3},{2,0},{3,1},{4,6},{5,7},{6,4},{7,5},{8,10},{9,11},{10,... | collective-permute-start | bytes 884744 | tf_op jit(solution)/shard_map/ppermute | solution.py:191
  47.2 19.8 %collective-permute-start.34 = (bf16[512,512]{1,0:T(8,128)(2,1)S(1)}, bf16[512,512]{1,0:T(8,128)(2,1)S(1)}, u32[]{:S(2)}, u32[]{:S(2)}) collective-permute-start(bf16[512,512]{1,0:T(8,128)(2,1)S(1)} %bitcast.19), channel_id=1, source_target_pairs={{0,2},{1,3},{2,0},{3,1},{4,6},{5,7},{6,4},{7,5},{8,10},{9,11},{10,... | collective-permute-start | bytes 1572872 | tf_op jit(solution)/shard_map/ppermute | solution.py:792
  48.6 2.1 collective-permute-start.30
  48.6 2.3 %collective-permute-start.33 = (bf16[64,2304]{1,0:T(8,128)(2,1)}, bf16[64,2304]{1,0:T(8,128)(2,1)}, u32[]{:S(2)}, u32[]{:S(2)}) collective-permute-start(bf16[64,2304]{1,0:T(8,128)(2,1)} %collective-permute-done.29.refs_3_), channel_id=1, source_target_pairs={{0,1},{1,0},{2,3},{3,2},{4,5},{5,4},{6,7},{7,6},{8,9},{9,8},{10,11... | collective-permute-start | bytes 884744 | tf_op jit(solution)/shard_map/ppermute | solution.py:191
  49.1 2.3 %collective-permute-start.32 = (bf16[64,2304]{1,0:T(8,128)(2,1)}, bf16[64,2304]{1,0:T(8,128)(2,1)}, u32[]{:S(2)}, u32[]{:S(2)}) collective-permute-start(bf16[64,2304]{1,0:T(8,128)(2,1)} %collective-permute-done.28.refs_2_), channel_id=1, source_target_pairs={{0,1},{1,0},{2,3},{3,2},{4,5},{5,4},{6,7},{7,6},{8,9},{9,8},{10,11... | collective-permute-start | bytes 884744 | tf_op jit(solution)/shard_map/ppermute | solution.py:191
  49.1 2.7 %collective-permute-start.31 = (bf16[64,2304]{1,0:T(8,128)(2,1)}, bf16[64,2304]{1,0:T(8,128)(2,1)}, u32[]{:S(2)}, u32[]{:S(2)}) collective-permute-start(bf16[64,2304]{1,0:T(8,128)(2,1)} %collective-permute-done.27.refs_1_), channel_id=1, source_target_pairs={{0,1},{1,0},{2,3},{3,2},{4,5},{5,4},{6,7},{7,6},{8,9},{9,8},{10,11... | collective-permute-start | bytes 884744 | tf_op jit(solution)/shard_map/ppermute | solution.py:191
  51.8 15.8 %copy-start.1 = (bf16[1,512,512]{2,1,0:T(8,128)(2,1)S(1)}, bf16[1,512,512]{2,1,0:T(8,128)(2,1)}, u32[]{:S(2)}) copy-start(bf16[1,512,512]{2,1,0:T(8,128)(2,1)} %param.42) | copy-start | bytes 1572868
  67.6 26.1 %all-to-all-start.1 = ((bf16[4,208,512]{2,1,0:T(8,128)(2,1)}), bf16[4,208,512]{2,1,0:T(8,128)(2,1)}, u32[]{:S(2)}, u32[]{:S(2)}) async-start(bf16[4,208,512]{2,1,0:T(8,128)(2,1)} %get-tuple-element.252), calls=%async_computation.1 | async-start | bytes 1703936 | tf_op jit(solution)/shard_map/cond/branch_1_fun/all_to_all | solution.py:916
  71.8 13.6 %collective-permute-start.24 = (bf16[512,512]{1,0:T(8,128)(2,1)S(1)}, bf16[512,512]{1,0:T(8,128)(2,1)}, u32[]{:S(2)}, u32[]{:S(2)}) collective-permute-start(bf16[512,512]{1,0:T(8,128)(2,1)S(1)} %get-tuple-element.262.refs_6_), channel_id=1, source_target_pairs={{0,2},{1,3},{2,0},{3,1},{4,6},{5,7},{6,4},{7,5},{8,10},{9,11},{10,... | collective-permute-start | bytes 1572872 | tf_op jit(solution)/shard_map/cond/branch_1_fun/ppermute | solution.py:792
  74.6 36.8 %collective-permute-start.21 = (bf16[4,192,512]{2,1,0:T(8,128)(2,1)}, bf16[4,192,512]{2,1,0:T(8,128)(2,1)}, u32[]{:S(2)}, u32[]{:S(2)}) collective-permute-start(bf16[4,192,512]{2,1,0:T(8,128)(2,1)} %dynamic-slice_bitcast_fusion), channel_id=1, source_target_pairs={{0,4},{4,0},{8,12},{12,8},{16,20},{20,16},{24,28},{28,24},{1,5},{5... | collective-permute-start | bytes 2359304 | tf_op jit(solution)/shard_map/cond/branch_1_fun/ppermute | solution.py:797
  76.1 9.3 %collective-permute-start.22 = (bf16[512,512]{1,0:T(8,128)(2,1)S(1)}, bf16[512,512]{1,0:T(8,128)(2,1)}, u32[]{:S(2)}, u32[]{:S(2)}) collective-permute-start(bf16[512,512]{1,0:T(8,128)(2,1)S(1)} %get-tuple-element.260.refs_2_), channel_id=1, source_target_pairs={{0,1},{1,0},{2,3},{3,2},{4,5},{5,4},{6,7},{7,6},{8,9},{9,8},{10,11... | collective-permute-start | bytes 1572872 | tf_op jit(solution)/shard_map/cond/branch_1_fun/ppermute | solution.py:792
  76.1 10.8 %collective-permute-start.23 = (bf16[512,512]{1,0:T(8,128)(2,1)S(1)}, bf16[512,512]{1,0:T(8,128)(2,1)}, u32[]{:S(2)}, u32[]{:S(2)}) collective-permute-start(bf16[512,512]{1,0:T(8,128)(2,1)S(1)} %get-tuple-element.261.refs_4_), channel_id=1, source_target_pairs={{0,1},{1,0},{2,3},{3,2},{4,5},{5,4},{6,7},{7,6},{8,9},{9,8},{10,11... | collective-permute-start | bytes 1572872 | tf_op jit(solution)/shard_map/cond/branch_1_fun/ppermute | solution.py:792
  76.6 12.0 %collective-permute-start.25 = (bf16[512,512]{1,0:T(8,128)(2,1)S(1)}, bf16[512,512]{1,0:T(8,128)(2,1)}, u32[]{:S(2)}, u32[]{:S(2)}) collective-permute-start(bf16[512,512]{1,0:T(8,128)(2,1)S(1)} %get-tuple-element.262.refs_6_), channel_id=1, source_target_pairs={{0,1},{1,0},{2,3},{3,2},{4,5},{5,4},{6,7},{7,6},{8,9},{9,8},{10,11... | collective-permute-start | bytes 1572872 | tf_op jit(solution)/shard_map/cond/branch_1_fun/ppermute | solution.py:792
  85.4 6.4 %collective-permute-start.26 = (bf16[512,512]{1,0:T(8,128)(2,1)}, bf16[512,512]{1,0:T(8,128)(2,1)}, u32[]{:S(2)}, u32[]{:S(2)}) collective-permute-start(bf16[512,512]{1,0:T(8,128)(2,1)} %collective-permute-done.24.refs_8_), channel_id=1, source_target_pairs={{0,1},{1,0},{2,3},{3,2},{4,5},{5,4},{6,7},{7,6},{8,9},{9,8},{10,11... | collective-permute-start | bytes 1572872 | tf_op jit(solution)/shard_map/cond/branch_1_fun/ppermute | solution.py:792
  85.4 26.0 %collective-permute-start.17 = (bf16[208,512]{1,0:T(8,128)(2,1)}, bf16[208,512]{1,0:T(8,128)(2,1)}, u32[]{:S(2)}, u32[]{:S(2)}) collective-permute-start(bf16[208,512]{1,0:T(8,128)(2,1)} %get-tuple-element.253), channel_id=1, source_target_pairs={{0,4},{4,0},{8,12},{12,8},{16,20},{20,16},{24,28},{28,24},{1,5},{5... | collective-permute-start | bytes 638984 | tf_op jit(solution)/shard_map/cond/branch_1_fun/ppermute | solution.py:797
  86.9 24.5 %collective-permute-start.18 = (bf16[208,512]{1,0:T(8,128)(2,1)}, bf16[208,512]{1,0:T(8,128)(2,1)}, u32[]{:S(2)}, u32[]{:S(2)}) collective-permute-start(bf16[208,512]{1,0:T(8,128)(2,1)} %get-tuple-element.254), channel_id=1, source_target_pairs={{0,12},{4,8},{8,4},{12,0},{16,28},{20,24},{24,20},{28,16},{1,13},{... | collective-permute-start | bytes 638984 | tf_op jit(solution)/shard_map/cond/branch_1_fun/ppermute | solution.py:797
  88.5 22.8 %collective-permute-start.19 = (bf16[208,512]{1,0:T(8,128)(2,1)}, bf16[208,512]{1,0:T(8,128)(2,1)}, u32[]{:S(2)}, u32[]{:S(2)}) collective-permute-start(bf16[208,512]{1,0:T(8,128)(2,1)} %get-tuple-element.255), channel_id=1, source_target_pairs={{0,20},{4,16},{8,28},{12,24},{16,4},{20,0},{24,12},{28,8},{1,21},{... | collective-permute-start | bytes 638984 | tf_op jit(solution)/shard_map/cond/branch_1_fun/ppermute | solution.py:797
  91.8 19.5 %collective-permute-start.20 = (bf16[208,512]{1,0:T(8,128)(2,1)}, bf16[208,512]{1,0:T(8,128)(2,1)}, u32[]{:S(2)}, u32[]{:S(2)}) collective-permute-start(bf16[208,512]{1,0:T(8,128)(2,1)} %get-tuple-element.256), channel_id=1, source_target_pairs={{0,28},{4,24},{8,20},{12,16},{16,12},{20,8},{24,4},{28,0},{1,29},{... | collective-permute-start | bytes 638984 | tf_op jit(solution)/shard_map/cond/branch_1_fun/ppermute | solution.py:797
  111.6 40.2 %all-to-all-start = ((bf16[4,208,512]{2,1,0:T(8,128)(2,1)}), bf16[4,208,512]{2,1,0:T(8,128)(2,1)}, u32[]{:S(2)}, u32[]{:S(2)}) async-start(bf16[4,208,512]{2,1,0:T(8,128)(2,1)} %get-tuple-element.281), calls=%async_computation | async-start | bytes 1703936 | tf_op jit(solution)/shard_map/cond/branch_1_fun/all_to_all | solution.py:916
  128.0 23.3 %collective-permute-start.1 = (bf16[208,512]{1,0:T(8,128)(2,1)}, bf16[208,512]{1,0:T(8,128)(2,1)}, u32[]{:S(2)}, u32[]{:S(2)}) collective-permute-start(bf16[208,512]{1,0:T(8,128)(2,1)} %get-tuple-element.297), channel_id=1, source_target_pairs={{0,4},{4,0},{8,12},{12,8},{16,20},{20,16},{24,28},{28,24},{1,5},{5... | collective-permute-start | bytes 638984 | tf_op jit(solution)/shard_map/cond/branch_1_fun/ppermute | solution.py:797
  129.5 21.8 %collective-permute-start.2 = (bf16[208,512]{1,0:T(8,128)(2,1)}, bf16[208,512]{1,0:T(8,128)(2,1)}, u32[]{:S(2)}, u32[]{:S(2)}) collective-permute-start(bf16[208,512]{1,0:T(8,128)(2,1)} %get-tuple-element.298), channel_id=1, source_target_pairs={{0,12},{4,8},{8,4},{12,0},{16,28},{20,24},{24,20},{28,16},{1,13},{... | collective-permute-start | bytes 638984 | tf_op jit(solution)/shard_map/cond/branch_1_fun/ppermute | solution.py:797
  131.5 20.2 %collective-permute-start.3 = (bf16[208,512]{1,0:T(8,128)(2,1)}, bf16[208,512]{1,0:T(8,128)(2,1)}, u32[]{:S(2)}, u32[]{:S(2)}) collective-permute-start(bf16[208,512]{1,0:T(8,128)(2,1)} %get-tuple-element.299), channel_id=1, source_target_pairs={{0,20},{4,16},{8,28},{12,24},{16,4},{20,0},{24,12},{28,8},{1,21},{... | collective-permute-start | bytes 638984 | tf_op jit(solution)/shard_map/cond/branch_1_fun/ppermute | solution.py:797
  134.8 16.9 %collective-permute-start.4 = (bf16[208,512]{1,0:T(8,128)(2,1)}, bf16[208,512]{1,0:T(8,128)(2,1)}, u32[]{:S(2)}, u32[]{:S(2)}) collective-permute-start(bf16[208,512]{1,0:T(8,128)(2,1)} %get-tuple-element.300), channel_id=1, source_target_pairs={{0,28},{4,24},{8,20},{12,16},{16,12},{20,8},{24,4},{28,0},{1,29},{... | collective-permute-start | bytes 638984 | tf_op jit(solution)/shard_map/cond/branch_1_fun/ppermute | solution.py:797
  145.9 2.9 %collective-permute-start = (bf16[1024,512]{1,0:T(8,128)(2,1)}, bf16[1024,512]{1,0:T(8,128)(2,1)S(1)}, u32[]{:S(2)}, u32[]{:S(2)}) collective-permute-start(bf16[1024,512]{1,0:T(8,128)(2,1)} %get-tuple-element.280), channel_id=1, source_target_pairs={{0,1},{1,0},{2,3},{3,2},{4,5},{5,4},{6,7},{7,6},{8,9},{9,8},{10,11... | collective-permute-start | bytes 3145736 | tf_op jit(solution)/shard_map/cond/branch_1_fun/cond/branch_1_fun/ppermute | solution.py:792
  151.9 6.5 %copy-start.3 = (f32[512,512]{1,0:T(8,128)S(1)}, f32[512,512]{1,0:T(8,128)}, u32[]{:S(2)}) copy-start(f32[512,512]{1,0:T(8,128)} %get-tuple-element.486) | copy-start | bytes 3145732
  151.9 6.5 %copy-start.4 = (bf16[512,512]{1,0:T(8,128)(2,1)S(1)}, bf16[512,512]{1,0:T(8,128)(2,1)}, u32[]{:S(2)}) copy-start(bf16[512,512]{1,0:T(8,128)(2,1)} %param.43) | copy-start | bytes 1572868
  151.9 6.5 %copy-start.5 = (bf16[512,512]{1,0:T(8,128)(2,1)S(1)}, bf16[512,512]{1,0:T(8,128)(2,1)}, u32[]{:S(2)}) copy-start(bf16[512,512]{1,0:T(8,128)(2,1)} %tokens_ref.1) | copy-start | bytes 1572868
  152.0 51.4 %all-to-all-start.3 = ((bf16[8,192,512]{2,1,0:T(8,128)(2,1)}), bf16[8,192,512]{2,1,0:T(8,128)(2,1)}, u32[]{:S(2)}, u32[]{:S(2)}) async-start(bf16[8,192,512]{2,1,0:T(8,128)(2,1)} %get-tuple-element.504), calls=%async_computation.3 | async-start | bytes 3145728 | tf_op jit(solution)/shard_map/all_to_all | solution.py:1009
  158.5 24.6 %collective-permute-start.6 = (bf16[1024,512]{1,0:T(8,128)(2,1)}, bf16[1024,512]{1,0:T(8,128)(2,1)}, u32[]{:S(2)}, u32[]{:S(2)}) collective-permute-start(bf16[1024,512]{1,0:T(8,128)(2,1)} %get-tuple-element.325), channel_id=1, source_target_pairs={{0,2},{1,3},{2,0},{3,1},{4,6},{5,7},{6,4},{7,5},{8,10},{9,11},{10,... | collective-permute-start | bytes 3145736 | tf_op jit(solution)/shard_map/cond/branch_1_fun/ppermute | solution.py:792
  178.5 3.3 %collective-permute-start.5 = (bf16[256,2304]{1,0:T(8,128)(2,1)}, bf16[256,2304]{1,0:T(8,128)(2,1)}, u32[]{:S(2)}, u32[]{:S(2)}) collective-permute-start(bf16[256,2304]{1,0:T(8,128)(2,1)} %get-tuple-element.324), channel_id=1, source_target_pairs={{0,1},{1,0},{2,3},{3,2},{4,5},{5,4},{6,7},{7,6},{8,9},{9,8},{10,11... | collective-permute-start | bytes 3538952 | tf_op jit(solution)/shard_map/cond/branch_1_fun/cond/branch_1_fun/ppermute | solution.py:191
  185.1 3.6 %copy-start.2 = (bf16[512,512]{1,0:T(8,128)(2,1)}, bf16[512,512]{1,0:T(8,128)(2,1)S(1)}, u32[]{:S(2)}) copy-start(bf16[512,512]{1,0:T(8,128)(2,1)S(1)} %get-tuple-element.359.refs_9_) | copy-start | bytes 1572868 | tf_op jit(solution)/shard_map/cond
  185.2 15.0 %collective-permute-start.7 = (bf16[64,2304]{1,0:T(8,128)(2,1)S(1)}, bf16[64,2304]{1,0:T(8,128)(2,1)}, u32[]{:S(2)}, u32[]{:S(2)}) collective-permute-start(bf16[64,2304]{1,0:T(8,128)(2,1)S(1)} %get-tuple-element.346), channel_id=1, source_target_pairs={{0,2},{1,3},{2,0},{3,1},{4,6},{5,7},{6,4},{7,5},{8,10},{9,11},{10,... | collective-permute-start | bytes 884744 | tf_op jit(solution)/shard_map/cond/branch_1_fun/ppermute | solution.py:191
  186.2 14.0 %collective-permute-start.8 = (bf16[64,2304]{1,0:T(8,128)(2,1)S(1)}, bf16[64,2304]{1,0:T(8,128)(2,1)}, u32[]{:S(2)}, u32[]{:S(2)}) collective-permute-start(bf16[64,2304]{1,0:T(8,128)(2,1)S(1)} %get-tuple-element.347), channel_id=1, source_target_pairs={{0,4},{1,5},{2,6},{3,7},{4,0},{5,1},{6,2},{7,3},{8,12},{9,13},{10,... | collective-permute-start | bytes 884744 | tf_op jit(solution)/shard_map/cond/branch_1_fun/ppermute | solution.py:191
  187.9 14.2 %collective-permute-start.9 = (bf16[64,2304]{1,0:T(8,128)(2,1)S(1)}, bf16[64,2304]{1,0:T(8,128)(2,1)}, u32[]{:S(2)}, u32[]{:S(2)}) collective-permute-start(bf16[64,2304]{1,0:T(8,128)(2,1)S(1)} %get-tuple-element.348), channel_id=1, source_target_pairs={{0,6},{1,7},{2,4},{3,5},{4,2},{5,3},{6,0},{7,1},{8,14},{9,15},{10,... | collective-permute-start | bytes 884744 | tf_op jit(solution)/shard_map/cond/branch_1_fun/ppermute | solution.py:191
  203.4 8.6 %collective-permute-start.13 = (bf16[1024,512]{1,0:T(8,128)(2,1)}, bf16[1024,512]{1,0:T(8,128)(2,1)S(1)}, u32[]{:S(2)}, u32[]{:S(2)}) collective-permute-start(bf16[1024,512]{1,0:T(8,128)(2,1)} %get-tuple-element.370), channel_id=1, source_target_pairs={{0,1},{1,0},{2,3},{3,2},{4,5},{5,4},{6,7},{7,6},{8,9},{9,8},{10,11... | collective-permute-start | bytes 3145736 | tf_op jit(solution)/shard_map/cond/branch_1_fun/ppermute | solution.py:792
  203.5 11.5 %collective-permute-start.10 = (bf16[16,2304]{1,0:T(8,128)(2,1)S(1)}, bf16[16,2304]{1,0:T(8,128)(2,1)}, u32[]{:S(2)}, u32[]{:S(2)}) collective-permute-start(bf16[16,2304]{1,0:T(8,128)(2,1)S(1)} %get-tuple-element.363), channel_id=1, source_target_pairs={{0,8},{1,9},{2,10},{3,11},{4,12},{5,13},{6,14},{7,15},{8,0},{9,1},... | collective-permute-start | bytes 221192 | tf_op jit(solution)/shard_map/cond/branch_1_fun/ppermute | solution.py:191
  206.8 8.8 %collective-permute-start.11 = (bf16[16,2304]{1,0:T(8,128)(2,1)S(1)}, bf16[16,2304]{1,0:T(8,128)(2,1)}, u32[]{:S(2)}, u32[]{:S(2)}) collective-permute-start(bf16[16,2304]{1,0:T(8,128)(2,1)S(1)} %get-tuple-element.364), channel_id=1, source_target_pairs={{0,16},{1,17},{2,18},{3,19},{4,20},{5,21},{6,22},{7,23},{8,24},{9,... | collective-permute-start | bytes 221192 | tf_op jit(solution)/shard_map/cond/branch_1_fun/ppermute | solution.py:191
  206.8 8.8 %collective-permute-start.12 = (bf16[16,2304]{1,0:T(8,128)(2,1)S(1)}, bf16[16,2304]{1,0:T(8,128)(2,1)}, u32[]{:S(2)}, u32[]{:S(2)}) collective-permute-start(bf16[16,2304]{1,0:T(8,128)(2,1)S(1)} %get-tuple-element.365), channel_id=1, source_target_pairs={{0,24},{1,25},{2,26},{3,27},{4,28},{5,29},{6,30},{7,31},{8,16},{9,... | collective-permute-start | bytes 221192 | tf_op jit(solution)/shard_map/cond/branch_1_fun/ppermute | solution.py:191
  215.6 1.8 copy-start.7
